TPU v7x, 128 devices: a whole 4x4x4 slice. The times are simulated.
128 devices in a mesh: dp: 16 (over x, z), tensor: 8 (over y, core).
Axes of the slice: x: 4, y: 4, z: 4, core: 2. Of those that a mesh axis runs over, the one named last changes fastest.
Arguments:
- queries: bfloat16 [16, 512, 8192], P('dp', None, 'tensor'), may hold values from -8 to 8
- new_keys: bfloat16 [16, 512, 512], P('dp', None, 'tensor'), may hold values from -8 to 8
- new_values: bfloat16 [16, 512, 512], P('dp', None, 'tensor'), may hold values from -6 to 6
- key_cache: bfloat16 [1024, 128, 512], P('dp', None, 'tensor'), may hold values from -8 to 8
- value_cache: bfloat16 [1024, 128, 512], P('dp', None, 'tensor'), may hold values from -6 to 6
- page_owner: int32 [32, 8, 1], replicated, may hold values from 0 to 15; in each aligned block of 16 rows (0 to 15, 16 to 31, ..., all dimensions but the last counted through in order) at most 4 rows name the same one
- page_slot: int32 [32, 8], replicated, may hold values from 0 to 63
- tile_req: int32 [96], replicated, may hold values from 0 to 15, as said below
- tile_node: int32 [96], replicated, may hold values from 0 to 31, as said below
- suffix_len: int32 [16], P('dp'), may hold values from 1 to 512, 6144 in all
Outputs:
- attended: bfloat16 [16, 512, 8192], P('dp', None, 'tensor')
Inputs may be any that keep to these rules, and one draw needn't show every extreme that they name: `page_owner`: in each aligned block of 16 entries (the nodes kept by one index of dp) no owner appears more than 4 times. `tile_req`: the 6 tiles of one index of dp, positions e * 6 onward, name different requests. `tile_node`: tile i names a node of index i // 6 of dp, one of i // 6 * 2 to i // 6 * 2 + 1, and every node is named by some tile.
All inputs are finite; a program needn't handle non-finite values. No bound on the sum of `suffix_len` on one device may be relied on, other than what follows from the above.
Results may differ from a plain program's by a relative error of at most 0.0038.
Values may be sent and summed in bfloat16 or wider, within the bound.
A program may use at most 128 MiB of HBM per device.

v0:
```python
import math

import jax
import jax.numpy as jnp
from jax import lax
from jax.sharding import PartitionSpec as P

HD = 128
CAP = 4


FLOOR_SCORE = -1e30


def from_partner(block, axis, apart):
    count = lax.axis_size(axis)
    route = []
    for low in range(count):
        high = low | 1 << apart
        if high != low and high < count:
            route += [(low, high), (high, low)]
    return lax.ppermute(block, axis, route)


def join_halves(own_half, other_half, tp_parity):
    first_half = jnp.where(tp_parity == 0, own_half, other_half)
    second_half = jnp.where(tp_parity == 0, other_half, own_half)
    return jnp.concatenate([first_half, second_half], axis=-1)


def softmax_part(query_rows, key_rows, value_rows, allowed, softmax_scale):
    score = (
        lax.dot_general(
            query_rows, key_rows, (((1,), (1,)), ((), ())), preferred_element_type=jnp.float32
        )
        * softmax_scale
    )
    if allowed is not None:
        score = jnp.where(allowed, score, FLOOR_SCORE)
    row_max = jnp.max(score, axis=-1)
    weight = jnp.exp(score - row_max[:, None])
    row_sum = jnp.sum(weight, axis=-1)
    mixed = jnp.dot(weight.astype(jnp.bfloat16), value_rows, preferred_element_type=jnp.float32)
    return (row_max, row_sum, mixed)


def head_loop(query_rows, key_rows, value_rows, allowed, softmax_scale):

    def one_head(head_index):
        single = lax.dynamic_index_in_dim(query_rows, head_index, 1, keepdims=False)
        return softmax_part(single, key_rows, value_rows, allowed, softmax_scale)

    row_max, row_sum, mixed = lax.map(one_head, jnp.arange(query_rows.shape[1]))
    return (row_max.T, row_sum.T, jnp.transpose(mixed, (1, 0, 2)))


def body(
    queries,
    new_keys,
    new_values,
    key_cache,
    value_cache,
    page_owner,
    page_slot,
    tile_req,
    tile_node,
    suffix_len,
):
    dp_size = lax.axis_size("dp")
    dp_index = lax.axis_index("dp")
    tp_parity = lax.axis_index("tensor") % 2
    req_local, suf_len, row_width = queries.shape
    head_count = row_width // HD
    col_width = key_cache.shape[2]
    page_len = key_cache.shape[1]
    node_pages = page_owner.shape[1]
    node_local = page_owner.shape[0] // dp_size
    tile_local = tile_req.shape[0] // dp_size
    entry_count = node_local * node_pages
    node_len = node_pages * page_len
    softmax_scale = 1.0 / math.sqrt(HD)
    owners = page_owner.reshape(dp_size, entry_count)
    slot_ids = page_slot.reshape(dp_size, entry_count)
    entry_order = jnp.arange(entry_count)
    is_earlier = entry_order[None, :] < entry_order[:, None]
    same_owner = owners[:, :, None] == owners[:, None, :]
    owner_rank = jnp.sum(same_owner & is_earlier[None], axis=2)
    chosen = (owners[:, :, None] == dp_index) & (
        owner_rank[:, :, None] == jnp.arange(CAP)[None, None, :]
    )
    picked = jnp.sum(jnp.where(chosen, slot_ids[:, :, None], 0), axis=1)
    filled = jnp.any(chosen, axis=1)[:, :, None, None]
    send_keys = jnp.where(filled, key_cache[picked], jnp.zeros((), key_cache.dtype))
    send_values = jnp.where(filled, value_cache[picked], jnp.zeros((), value_cache.dtype))
    other_keys, other_values = from_partner((new_keys, new_values), "tensor", 0)
    fresh_keys = join_halves(new_keys, other_keys, tp_parity)
    fresh_values = join_halves(new_values, other_values, tp_parity)
    got_keys, got_values = (
        lax.all_to_all(send_keys, "dp", split_axis=0, concat_axis=0, tiled=True),
        lax.all_to_all(send_values, "dp", split_axis=0, concat_axis=0, tiled=True),
    )
    my_owner = lax.dynamic_index_in_dim(owners, dp_index, 0, keepdims=False)
    my_rank = lax.dynamic_index_in_dim(owner_rank, dp_index, 0, keepdims=False)
    node_keys = got_keys[my_owner, my_rank].reshape(node_local, node_len, col_width)
    node_values = got_values[my_owner, my_rank].reshape(node_local, node_len, col_width)
    position = jnp.arange(suf_len)

    def own_suffix(request):
        query_rows = queries[request].reshape(suf_len, head_count, HD)
        allowed = (position[None, :] <= position[:, None]) & (
            position[None, :] < suffix_len[request]
        )
        return head_loop(
            query_rows, fresh_keys[request], fresh_values[request], allowed, softmax_scale
        )

    self_max, self_sum, self_out = lax.map(own_suffix, jnp.arange(req_local))
    far_keys, far_values = from_partner((node_keys, node_values), "tensor", 0)
    node_keys = join_halves(node_keys, far_keys, tp_parity)
    node_values = join_halves(node_values, far_values, tp_parity)

    def tile_part(query_flat, key_rows, value_rows):
        row_max, row_sum, mixed = head_loop(
            query_flat.reshape(suf_len, head_count, HD), key_rows, value_rows, None, softmax_scale
        )
        return (row_max, row_sum, mixed.reshape(suf_len, head_count * HD).astype(jnp.bfloat16))

    requests = lax.dynamic_slice_in_dim(tile_req, dp_index * tile_local, tile_local)
    tile_nodes = (
        lax.dynamic_slice_in_dim(tile_node, dp_index * tile_local, tile_local)
        - dp_index * node_local
    )
    target = requests // req_local
    seat_index = requests % req_local
    everyone = lax.all_gather(queries, "dp", axis=0, tiled=True)

    def run_tile(tile_index):
        node_pick = tile_nodes[tile_index]
        return tile_part(
            everyone[requests[tile_index]], node_keys[node_pick], node_values[node_pick]
        )

    tile_max, tile_sum, tile_out = lax.map(run_tile, jnp.arange(tile_local))
    max_buffer = jnp.full((dp_size, req_local, suf_len, head_count), FLOOR_SCORE, jnp.float32)
    max_buffer = max_buffer.at[target, seat_index].set(tile_max)
    sum_buffer = jnp.zeros((dp_size, req_local, suf_len, head_count), jnp.float32)
    sum_buffer = sum_buffer.at[target, seat_index].set(tile_sum)
    out_buffer = jnp.zeros((dp_size, req_local, suf_len, head_count * HD), jnp.bfloat16)
    out_buffer = out_buffer.at[target, seat_index].set(tile_out)
    far_max, far_sum = (
        lax.all_to_all(max_buffer, "dp", split_axis=0, concat_axis=0, tiled=True),
        lax.all_to_all(sum_buffer, "dp", split_axis=0, concat_axis=0, tiled=True),
    )
    far_out = lax.all_to_all(out_buffer, "dp", split_axis=0, concat_axis=0, tiled=True)
    global_max = jnp.maximum(self_max, jnp.max(far_max, axis=0))
    self_factor = jnp.exp(self_max - global_max)
    far_factor = jnp.exp(far_max - global_max[None])
    row_sum = self_sum * self_factor + jnp.sum(far_sum * far_factor, axis=0)

    def add_holder(holder_index, running):
        holder_rows = (
            far_out[holder_index].reshape(req_local, suf_len, head_count, HD).astype(jnp.float32)
        )
        return running + holder_rows * far_factor[holder_index][..., None]

    mixed = lax.fori_loop(0, dp_size, add_holder, self_out * self_factor[..., None])
    is_valid = position[None, :] < suffix_len[:, None]
    result = jnp.where(is_valid[:, :, None, None], mixed / row_sum[..., None], 0.0)
    return result.reshape(req_local, suf_len, head_count * HD).astype(jnp.bfloat16)


def solution(mesh):
    return jax.shard_map(
        body,
        mesh=mesh,
        in_specs=(
            P("dp", None, "tensor"),
            P("dp", None, "tensor"),
            P("dp", None, "tensor"),
            P("dp", None, "tensor"),
            P("dp", None, "tensor"),
            P(),
            P(),
            P(),
            P(),
            P("dp"),
        ),
        out_specs=P("dp", None, "tensor"),
        check_vma=False,
    )
```

profile of v0, /device:TPU:0, one launch (start us, length us, event | category | flops | bytes accessed | tf_op | source)
XLA Modules:
  0.0 850.7 jit_solution(9025616519533283018)
XLA Ops:
  13.2 33.4 %all_to_all.25 = bf16[16,4,128,64]{2,3,1,0:T(8,128)(2,1)S(1)} all-to-all(bf16[16,4,128,64]{2,3,1,0:T(8,128)(2,1)S(1)} %get-tuple-element.469), channel_id=1, replica_groups=mesh['dp'=16,'tensor'=8] {'dp'}, dimensions={0} | all-to-all | bytes 2097152 | tf_op jit(solution)/shard_map/all_to_all | solution.py:100
  46.6 5.3 all-to-all-start
  52.9 13.2 %all-to-all-done = bf16[16,4,128,64]{2,3,1,0:T(8,128)(2,1)S(1)} async-done(((bf16[16,4,128,64]{2,3,1,0:T(8,128)(2,1)}), bf16[16,4,128,64]{2,3,1,0:T(8,128)(2,1)S(1)}, u32[]{:S(2)}, u32[]{:S(2)}) %all-to-all-start) | async-done | bytes 1048608 | tf_op jit(solution)/shard_map/all_to_all | solution.py:99
  71.2 64.7 %all-gather.2.cloned.1.call-done = bf16[16,512,1024]{2,1,0:T(8,128)(2,1)} async-done(((bf16[1,512,1024]{2,1,0:T(8,128)(2,1)}), bf16[16,512,1024]{2,1,0:T(8,128)(2,1)}) %all-gather.2.cloned.1.call-update) | async-done | bytes 16777232 | tf_op jit(solution)/shard_map/all_gather | solution.py:135
  135.9 275.9 %while.68 = (s32[]{:T(128)}, f32[6,512,8]{1,2,0:T(8,128)S(1)}, f32[6,512,8]{1,2,0:T(8,128)S(1)}, bf16[6,512,1024]{2,1,0:T(8,128)(2,1)}, s32[6]{0:T(128)S(1)}, /*...) while((s32[]{:T(128)}, f32[6,512,8]{1,2,0:T(8,128)S(1)}, ...), condition=%wide.region_12.13_spmd, body=%wide.region_7.12_spmd.sunk | while | flops 272628736 | bytes 27215064 | solution.py:143
  145.3 34.3 %while.71 = (s32[]{:T(128)}, f32[8,512]{1,0:T(8,128)S(1)}, f32[8,512]{1,0:T(8,128)S(1)}, bf16[8,512,128]{2,1,0:T(8,128)(2,1)S(1)}, s32[8]{0:T(128)S(1)}, /*index...) while((s32[]{:T(128)}, f32[8,512]{1,0:T(8,128)S(1)}, ...), condition=%wide.region_11.11_spmd, body=%wide.region_8.10_spmd.sunk | while | flops 272628736 | bytes 7225515 | solution.py:53
  191.3 34.3 %while.71 = (s32[]{:T(128)}, f32[8,512]{1,0:T(8,128)S(1)}, f32[8,512]{1,0:T(8,128)S(1)}, bf16[8,512,128]{2,1,0:T(8,128)(2,1)S(1)}, s32[8]{0:T(128)S(1)}, /*index...) while((s32[]{:T(128)}, f32[8,512]{1,0:T(8,128)S(1)}, ...), condition=%wide.region_11.11_spmd, body=%wide.region_8.10_spmd.sunk | while | flops 272628736 | bytes 7225515 | solution.py:53
  237.3 34.3 %while.71 = (s32[]{:T(128)}, f32[8,512]{1,0:T(8,128)S(1)}, f32[8,512]{1,0:T(8,128)S(1)}, bf16[8,512,128]{2,1,0:T(8,128)(2,1)S(1)}, s32[8]{0:T(128)S(1)}, /*index...) while((s32[]{:T(128)}, f32[8,512]{1,0:T(8,128)S(1)}, ...), condition=%wide.region_11.11_spmd, body=%wide.region_8.10_spmd.sunk | while | flops 272628736 | bytes 7225515 | solution.py:53
  283.3 34.3 %while.71 = (s32[]{:T(128)}, f32[8,512]{1,0:T(8,128)S(1)}, f32[8,512]{1,0:T(8,128)S(1)}, bf16[8,512,128]{2,1,0:T(8,128)(2,1)S(1)}, s32[8]{0:T(128)S(1)}, /*index...) while((s32[]{:T(128)}, f32[8,512]{1,0:T(8,128)S(1)}, ...), condition=%wide.region_11.11_spmd, body=%wide.region_8.10_spmd.sunk | while | flops 272628736 | bytes 7225515 | solution.py:53
  329.3 34.3 %while.71 = (s32[]{:T(128)}, f32[8,512]{1,0:T(8,128)S(1)}, f32[8,512]{1,0:T(8,128)S(1)}, bf16[8,512,128]{2,1,0:T(8,128)(2,1)S(1)}, s32[8]{0:T(128)S(1)}, /*index...) while((s32[]{:T(128)}, f32[8,512]{1,0:T(8,128)S(1)}, ...), condition=%wide.region_11.11_spmd, body=%wide.region_8.10_spmd.sunk | while | flops 272628736 | bytes 7225515 | solution.py:53
  375.3 34.3 %while.71 = (s32[]{:T(128)}, f32[8,512]{1,0:T(8,128)S(1)}, f32[8,512]{1,0:T(8,128)S(1)}, bf16[8,512,128]{2,1,0:T(8,128)(2,1)S(1)}, s32[8]{0:T(128)S(1)}, /*index...) while((s32[]{:T(128)}, f32[8,512]{1,0:T(8,128)S(1)}, ...), condition=%wide.region_11.11_spmd, body=%wide.region_8.10_spmd.sunk | while | flops 272628736 | bytes 7225515 | solution.py:53
  414.6 5.2 all-to-all-start.2
  422.6 5.8 all-to-all-done.2
  428.4 3.6 all-to-all-start.4
  432.0 6.0 broadcast.209
  438.0 16.1 %scatter_fusion.1 = bf16[16,512,1024]{2,1,0:T(8,128)(2,1)} fusion(bf16[16,512,1024]{2,1,0:T(8,128)(2,1)} %broadcast.209, s32[6]{0:T(128)S(1)} %get-tuple-element.453, bf16[6,512,1024]{2,1,0:T(8,128)(2,1)} %get-tuple-element.261), kind=kCustom, calls=%fused_computation.5 | custom fusion | bytes 18874392 | tf_op jit(solution)/shard_map/scatter | solution.py:149
  454.8 7.4 all-to-all-start.3
  467.7 58.0 %while.70 = (s32[]{:T(128)}, f32[8,512]{1,0:T(8,128)}, f32[8,512]{1,0:T(8,128)}, f32[8,512,128]{2,1,0:T(8,128)S(1)}, s32[8]{0:T(128)S(1)}, /*index=5*/bf16[512,8...) while((s32[]{:T(128)}, f32[8,512]{1,0:T(8,128)}, ...), condition=%wide.region_3.4_spmd.clone, body=%wide.region_0.0_spmd.clone.sunk | while | flops 136576000 | bytes 3818163 | solution.py:53
  531.5 226.7 %all-to-all-done.3 = bf16[16,1,512,1024]{3,2,1,0:T(8,128)(2,1)} async-done(((bf16[16,1,512,1024]{3,2,1,0:T(8,128)(2,1)}), bf16[16,1,512,1024]{3,2,1,0:T(8,128)(2,1)}, u32[]{:S(2)}, u32[]{:S(2)}) %all-to-all-start.3) | async-done | bytes 16777248 | tf_op jit(solution)/shard_map/all_to_all | solution.py:154
  758.3 80.7 %while.69 = (s32[]{:T(128)}, f32[1,512,8,128]{3,2,1,0:T(8,128)}, bf16[16,1,512,1024]{3,2,1,0:T(8,128)(2,1)}, f32[16,1,512,8]{2,3,1,0:T(8,128)S(1)}, s32[]{:T(128)}) while((s32[]{:T(128)}, f32[1,512,8,128]{3,2,1,0:T(8,128)}, bf16[16,1,512,1024]{3,2,1,0:T(8,128)(2,1)}, f32[16,1,512,8]{2,3,1,0:T(8,128)S(1)}, s32[]{:T(128)}) %tuple.121), condition=%wide.region_17.18_spmd, body=%wide.region_16.17_spmd.sunk | while | flops 1572866 | bytes 13713477 | solution.py:166
  765.4 2.9 fusion.53
  775.5 2.9 fusion.53
  785.6 2.9 fusion.53
  839.0 3.6 select_convert_fusion
  (637 shorter events, 294.1 us)
Async XLA Ops:
  6.5 129.3 %all-gather.2.cloned.1.call-start = ((), (), s32[]{:S(2)}) async-start(), calls=%async_computation.5 | async-start | bytes 17825792 | tf_op jit(solution)/shard_map/all_gather | solution.py:135
  46.6 19.6 %all-to-all-start = ((bf16[16,4,128,64]{2,3,1,0:T(8,128)(2,1)}), bf16[16,4,128,64]{2,3,1,0:T(8,128)(2,1)S(1)}, u32[]{:S(2)}, u32[]{:S(2)}) async-start(bf16[16,4,128,64]{2,3,1,0:T(8,128)(2,1)} %get-tuple-element.470), calls=%async_computation | async-start | bytes 2097152 | tf_op jit(solution)/shard_map/all_to_all | solution.py:99
  51.9 15.2 %copy-start.11 = (s32[96]{0:T(128)S(1)}, s32[96]{0:T(128)}, u32[]{:S(2)}) copy-start(s32[96]{0:T(128)} %param.25) | copy-start | bytes 1156
  51.9 15.2 %copy-start.12 = (s32[96]{0:T(128)S(1)}, s32[96]{0:T(128)}, u32[]{:S(2)}) copy-start(s32[96]{0:T(128)} %param.26) | copy-start | bytes 1156
  52.8 14.4 %collective-permute-start.3 = (bf16[2,1024,64]{1,0,2:T(2,128)(2,1)S(1)}, bf16[2,1024,64]{1,0,2:T(2,128)(2,1)S(1)}, u32[]{:S(2)}, u32[]{:S(2)}) collective-permute-start(bf16[2,1024,64]{1,0,2:T(2,128)(2,1)S(1)} %reshape.194), channel_id=1, source_target_pairs={{0,1},{1,0},{2,3},{3,2},{4,5},{5,4},{6,7},{7,6},{8,9},{9,8},{10,11... | collective-permute-start | bytes 786440 | tf_op jit(solution)/shard_map/ppermute | solution.py:22
  67.0 1.6 collective-permute-start.2
  135.9 9.3 %copy-start.2 = (bf16[2,1024,128]{2,1,0:T(8,128)(2,1)}, bf16[2,1024,128]{2,1,0:T(8,128)(2,1)S(1)}, u32[]{:S(2)}) copy-start(bf16[2,1024,128]{2,1,0:T(8,128)(2,1)S(1)} %get-tuple-element.819) | copy-start | bytes 1572868 | tf_op jit(solution)/shard_map/while
  135.9 9.3 %copy-start.4 = (bf16[2,1024,128]{2,1,0:T(8,128)(2,1)}, bf16[2,1024,128]{2,1,0:T(8,128)(2,1)S(1)}, u32[]{:S(2)}) copy-start(bf16[2,1024,128]{2,1,0:T(8,128)(2,1)S(1)} %get-tuple-element.818) | copy-start | bytes 1572868 | tf_op jit(solution)/shard_map/while
  181.8 9.3 %copy-start.2 = (bf16[2,1024,128]{2,1,0:T(8,128)(2,1)}, bf16[2,1024,128]{2,1,0:T(8,128)(2,1)S(1)}, u32[]{:S(2)}) copy-start(bf16[2,1024,128]{2,1,0:T(8,128)(2,1)S(1)} %get-tuple-element.819) | copy-start | bytes 1572868 | tf_op jit(solution)/shard_map/while
  181.8 9.3 %copy-start.4 = (bf16[2,1024,128]{2,1,0:T(8,128)(2,1)}, bf16[2,1024,128]{2,1,0:T(8,128)(2,1)S(1)}, u32[]{:S(2)}) copy-start(bf16[2,1024,128]{2,1,0:T(8,128)(2,1)S(1)} %get-tuple-element.818) | copy-start | bytes 1572868 | tf_op jit(solution)/shard_map/while
  227.9 9.3 %copy-start.2 = (bf16[2,1024,128]{2,1,0:T(8,128)(2,1)}, bf16[2,1024,128]{2,1,0:T(8,128)(2,1)S(1)}, u32[]{:S(2)}) copy-start(bf16[2,1024,128]{2,1,0:T(8,128)(2,1)S(1)} %get-tuple-element.819) | copy-start | bytes 1572868 | tf_op jit(solution)/shard_map/while
  227.9 9.3 %copy-start.4 = (bf16[2,1024,128]{2,1,0:T(8,128)(2,1)}, bf16[2,1024,128]{2,1,0:T(8,128)(2,1)S(1)}, u32[]{:S(2)}) copy-start(bf16[2,1024,128]{2,1,0:T(8,128)(2,1)S(1)} %get-tuple-element.818) | copy-start | bytes 1572868 | tf_op jit(solution)/shard_map/while
  273.9 9.3 %copy-start.2 = (bf16[2,1024,128]{2,1,0:T(8,128)(2,1)}, bf16[2,1024,128]{2,1,0:T(8,128)(2,1)S(1)}, u32[]{:S(2)}) copy-start(bf16[2,1024,128]{2,1,0:T(8,128)(2,1)S(1)} %get-tuple-element.819) | copy-start | bytes 1572868 | tf_op jit(solution)/shard_map/while
  273.9 9.3 %copy-start.4 = (bf16[2,1024,128]{2,1,0:T(8,128)(2,1)}, bf16[2,1024,128]{2,1,0:T(8,128)(2,1)S(1)}, u32[]{:S(2)}) copy-start(bf16[2,1024,128]{2,1,0:T(8,128)(2,1)S(1)} %get-tuple-element.818) | copy-start | bytes 1572868 | tf_op jit(solution)/shard_map/while
  319.9 9.3 %copy-start.2 = (bf16[2,1024,128]{2,1,0:T(8,128)(2,1)}, bf16[2,1024,128]{2,1,0:T(8,128)(2,1)S(1)}, u32[]{:S(2)}) copy-start(bf16[2,1024,128]{2,1,0:T(8,128)(2,1)S(1)} %get-tuple-element.819) | copy-start | bytes 1572868 | tf_op jit(solution)/shard_map/while
  319.9 9.3 %copy-start.4 = (bf16[2,1024,128]{2,1,0:T(8,128)(2,1)}, bf16[2,1024,128]{2,1,0:T(8,128)(2,1)S(1)}, u32[]{:S(2)}) copy-start(bf16[2,1024,128]{2,1,0:T(8,128)(2,1)S(1)} %get-tuple-element.818) | copy-start | bytes 1572868 | tf_op jit(solution)/shard_map/while
  365.8 9.3 %copy-start.2 = (bf16[2,1024,128]{2,1,0:T(8,128)(2,1)}, bf16[2,1024,128]{2,1,0:T(8,128)(2,1)S(1)}, u32[]{:S(2)}) copy-start(bf16[2,1024,128]{2,1,0:T(8,128)(2,1)S(1)} %get-tuple-element.819) | copy-start | bytes 1572868 | tf_op jit(solution)/shard_map/while
  365.8 9.3 %copy-start.4 = (bf16[2,1024,128]{2,1,0:T(8,128)(2,1)}, bf16[2,1024,128]{2,1,0:T(8,128)(2,1)S(1)}, u32[]{:S(2)}) copy-start(bf16[2,1024,128]{2,1,0:T(8,128)(2,1)S(1)} %get-tuple-element.818) | copy-start | bytes 1572868 | tf_op jit(solution)/shard_map/while
  414.6 13.8 %all-to-all-start.2 = ((f32[16,1,512,8]{2,3,1,0:T(8,128)}), f32[16,1,512,8]{2,3,1,0:T(8,128)S(1)}, u32[]{:S(2)}, u32[]{:S(2)}) async-start(f32[16,1,512,8]{2,3,1,0:T(8,128)} %bitcast.30), calls=%async_computation.2 | async-start | bytes 524288 | tf_op jit(solution)/shard_map/all_to_all | solution.py:151
  428.4 25.7 %all-to-all-start.4 = ((f32[16,1,512,8]{2,3,1,0:T(8,128)}), f32[16,1,512,8]{2,3,1,0:T(8,128)S(1)}, u32[]{:S(2)}, u32[]{:S(2)}) async-start(f32[16,1,512,8]{2,3,1,0:T(8,128)} %bitcast.35), calls=%async_computation.4 | async-start | bytes 524288 | tf_op jit(solution)/shard_map/all_to_all | solution.py:152
  454.8 8.9 %copy-start.7 = (bf16[1,512,1024]{2,1,0:T(8,128)(2,1)S(1)}, bf16[1,512,1024]{2,1,0:T(8,128)(2,1)}, u32[]{:S(2)}) copy-start(bf16[1,512,1024]{2,1,0:T(8,128)(2,1)} %param.18) | copy-start | bytes 3145732
  454.8 303.5 %all-to-all-start.3 = ((bf16[16,1,512,1024]{3,2,1,0:T(8,128)(2,1)}), bf16[16,1,512,1024]{3,2,1,0:T(8,128)(2,1)}, u32[]{:S(2)}, u32[]{:S(2)}) async-start(bf16[16,1,512,1024]{3,2,1,0:T(8,128)(2,1)} %bitcast.175), calls=%async_computation.3 | async-start | bytes 33554432 | tf_op jit(solution)/shard_map/all_to_all | solution.py:154
  462.4 3.3 collective-permute-start
  463.2 2.5 collective-permute-start.1
  (18 other events, 44.2 us)
Sparse Core Ops, SparseCore 0:
  9.5 126.3 all-gather.1
where the time goes:
time: 858 us; the launch traced here: 851 us
  waiting for transfers between devices  313 us (36%)
  local copies, waits for them, and re-layouts  148 us (17%)
  loops' own time  142 us (17%)
  other arithmetic  110 us (13%)
  matrix products  68.5 us (8%)
  blocking collectives  33.4 us (4%)
  starting transfers between devices  22.4 us (3%)
  between operations  14.4 us (2%)
    all_to_all x1, waiting for transfers between devices, body(): lax.all_to_all(out_buffer, 'dp', split_axis=0, concat_axis=0, tiled=True)  227 us
    another operation x7, loops' own time, head_loop(): row_max, row_sum, mixed = lax.map(one_head, jnp.arange(query_rows.shape[1]))  107 us
    all_gather x1, waiting for transfers between devices, body(): everyone = lax.all_gather(queries, 'dp', axis=0, tiled=True)  64.7 us
    add x16, other arithmetic, add_holder(): return running + holder_rows * far_factor[holder_index][..., None]  47.1 us
    dot_general x56, matrix products, softmax_part(): lax.dot_general(query_rows, key_rows, (((1,), (1,)), ((), ())), preferred...  36.9 us
    another operation x1, loops' own time, body(): tile_max, tile_sum, tile_out = lax.map(run_tile, jnp.arange(tile_local))  34.3 us
    dynamic_slice x56, local copies, waits for them, and re-layouts, head_loop(): row_max, row_sum, mixed = lax.map(one_head, jnp.arange(query_rows.shape[1]))  33.9 us
    all_to_all x1, blocking collectives, body(): lax.all_to_all(send_values, 'dp', split_axis=0, concat_axis=0, tiled=True)  33.4 us
  transfers between devices with their start and end apart: 9, of which 5 were waited for; matrix products, arithmetic and copies ran while one was open for 10% of the time, Pallas kernels for 0%

commit v1 on v0

v1 whole, which is shorter than its diff:
```python
import functools
import math

import jax
import jax.numpy as jnp
from jax import lax
from jax.experimental import pallas as pl
from jax.experimental.pallas import tpu as pltpu
from jax.sharding import PartitionSpec as P

HD = 128
CAP = 4
SIDE = 4
FLOOR_SCORE = -1e30
SCALE = 1.0 / math.sqrt(HD)
LOG2E = math.log2(math.e)
MESH = pl.DeviceIdType.MESH
MIB = 1 << 20


def from_partner(block):
    return lax.ppermute(block, "tensor", [(i, i ^ 1) for i in range(lax.axis_size("tensor"))])


def neighbour(me, axis, step):
    slow, fast = me // SIDE, me % SIDE
    if axis == 0:
        return lax.rem(slow + step, SIDE) * SIDE + fast
    return slow * SIDE + lax.rem(fast + step, SIDE)


def exchange_kernel(axis, with_small, *refs):
    if with_small:
        x_ref, y_ref, o_ref, oy_ref, mid, rel, s1, r1, s2, r2, lsem, ys, yr = refs
    else:
        x_ref, o_ref, mid, rel, s1, r1, s2, r2, lsem = refs
    me, t = lax.axis_index("dp"), lax.axis_index("tensor")
    place = (me // SIDE, me % SIDE)
    n = x_ref.shape[2 + axis] // 4

    def crd(a, k):
        return lax.rem(place[a] + k, SIDE)

    def cut(ref, start, size):
        return ref.at[:, start : start + size, :] if axis == 0 else ref.at[:, :, start : start + size]

    def quarter(ref, half, sub):
        return cut(ref, half * 2 * n, 2 * n) if sub is None else cut(ref, (half * 2 + sub) * n, n)

    def part(ref, sub):
        return ref if sub is None else cut(ref, sub * n, n)

    barrier = pltpu.get_barrier_semaphore()
    if with_small:
        for k in range(1, 16):
            pl.semaphore_signal(barrier, inc=1, device_id=(lax.rem(me + k, 16), t), device_id_type=MESH)
        pl.semaphore_wait(barrier, 15)
    else:
        for a in (0, 1):
            for k in (1, 3):
                pl.semaphore_signal(barrier, inc=1, device_id=(neighbour(me, a, k), t), device_id_type=MESH)
        pl.semaphore_wait(barrier, 4)

    def copy(src, dst, ss, rs, a, k):
        c = pltpu.make_async_remote_copy(
            src_ref=src, dst_ref=dst, send_sem=ss, recv_sem=rs, device_id=(neighbour(me, a, k), t), device_id_type=MESH
        )
        c.start()
        return c

    def phase(source, target, ss, rs, swap, relay):
        far, near = [], []
        for h in (0, 1):
            a = 1 - h if swap else h
            for j, k in ((0, 1), (1, 3)):
                far.append((h, j, k, copy(source(h, crd(a, 2), j), relay.at[h, j], ss.at[h, 0, j], rs.at[h, 0, j], a, k)))
            for j, k in ((0, 1), (1, 3)):
                near.append(copy(source(h, crd(a, k), None), target(h, crd(a, 0), None), ss.at[h, 1, j], rs.at[h, 1, j], a, k))
        for h, j, k, c in far:
            a = 1 - h if swap else h
            c.wait_recv()
            near.append(copy(relay.at[h, j], target(h, crd(a, 4 - k), j), ss.at[h, 2, j], rs.at[h, 2, j], a, k))
        for _, _, _, c in far:
            c.wait_send()
        return near

    def slab(ref, h, i):
        return ref.at[i] if h == 0 else ref.at[:, i]

    small = []
    if with_small:
        for k in range(1, 16):
            d = lax.rem(me + k, 16)
            c = pltpu.make_async_remote_copy(
                src_ref=y_ref.at[d], dst_ref=oy_ref.at[me], send_sem=ys.at[k], recv_sem=yr.at[k], device_id=(d, t), device_id_type=MESH
            )
            c.start()
            small.append(c)
        c = pltpu.make_async_copy(y_ref.at[me], oy_ref.at[me], ys.at[0])
        c.start()
        small.append(c)
    own = []
    for h in (0, 1):
        c = pltpu.make_async_copy(quarter(slab(x_ref, h, crd(h, 0)), h, None), mid.at[h, crd(h, 0)], lsem.at[h])
        c.start()
        own.append(c)
    flying = phase(
        lambda h, i, sub: quarter(slab(x_ref, h, i), h, sub), lambda h, i, sub: part(mid.at[h, i], sub), s1, r1, False, rel.at[0]
    )
    for c in own + flying:
        c.wait()

    def landing(h, b, sub):
        return quarter(o_ref.at[:, b] if h == 0 else o_ref.at[b], h, sub)

    own = []
    for h in (0, 1):
        b = crd(1 - h, 0)
        c = pltpu.make_async_copy(mid.at[h, :, b], landing(h, b, None), lsem.at[2 + h])
        c.start()
        own.append(c)
    flying = phase(lambda h, i, sub: part(mid.at[h, :, i], sub), landing, s2, r2, True, rel.at[1])
    for c in own + flying + small:
        c.wait()


def exchange(x, axis, collective_id, small=None):
    rows, lanes = x.shape[2:]
    half = (rows // 2, lanes) if axis == 0 else (rows, lanes // 2)
    sub = (rows // 4, lanes) if axis == 0 else (rows, lanes // 4)
    anywhere = pl.BlockSpec(memory_space=pl.ANY)
    args = (x,) if small is None else (x, small)
    scratch = [
        pltpu.VMEM((2, SIDE, SIDE) + half, x.dtype),
        pltpu.VMEM((2, 2, 2, SIDE) + sub, x.dtype),
        *[pltpu.SemaphoreType.DMA((2, 3, 2)) for _ in range(4)],
        pltpu.SemaphoreType.DMA((4,)),
    ]
    if small is not None:
        scratch += [pltpu.SemaphoreType.DMA((16,)), pltpu.SemaphoreType.DMA((16,))]
    out = pl.pallas_call(
        functools.partial(exchange_kernel, axis, small is not None),
        out_shape=[jax.ShapeDtypeStruct(a.shape, a.dtype) for a in args],
        in_specs=[anywhere] * len(args),
        out_specs=[anywhere] * len(args),
        scratch_shapes=scratch,
        compiler_params=pltpu.CompilerParams(collective_id=collective_id, has_side_effects=True, vmem_limit_bytes=32 * MIB),
    )(*args)
    return out[0] if small is None else out


def tiles_kernel(with_compute, tile_ref, slot_ref, own_ref, q_ref, o_ref, lse_ref, *scratch):
    blocks = scratch[:16]
    q_cols, k_rows, v_cols, part, part_max, acc, acc_max, ss, rs, ps, pr, lsem = scratch[16:]
    me, t = lax.axis_index("dp"), lax.axis_index("tensor")
    core = lax.rem(t, 2)
    mate = t + 1 - 2 * core
    place = (me // SIDE, me % SIDE)

    barrier = pltpu.get_barrier_semaphore()
    for a in (0, 1):
        for k in (1, 3):
            pl.semaphore_signal(barrier, inc=1, device_id=(neighbour(me, a, k), t), device_id_type=MESH)
    pl.semaphore_signal(barrier, inc=1, device_id=(me, mate), device_id_type=MESH)
    pl.semaphore_wait(barrier, 5)

    def number(h, i, j):
        i, j = i % SIDE, j % SIDE
        return i * SIDE + j if h == 0 else j * SIDE + i

    def block(h, i, j, kind):
        ref = blocks[number(h, i, j)].at[h, core]
        return ref if kind is None else ref.at[kind]

    sends, recvs, mates = [], {}, {}

    def send(h, i, j, first, k, kind=None):
        to = (i - k, j) if first else (i, j - k)
        a = h if first else 1 - h
        w = 0 if kind is None else kind
        src = own_ref.at[h] if (i, j) == (0, 0) else block(h, i, j, kind)
        c = pltpu.make_async_remote_copy(
            src_ref=src,
            dst_ref=block(h, *to, kind),
            send_sem=ss.at[h, number(h, *to), w],
            recv_sem=rs.at[h, number(h, *to), w],
            device_id=(neighbour(me, a, k), t),
            device_id_type=MESH,
        )
        c.start()
        sends.append(c)
        recvs[h, to[0] % SIDE, to[1] % SIDE, kind] = c

    def to_mate(h, i, j, kind=None):
        w = 0 if kind is None else kind
        src = own_ref.at[h] if (i, j) == (0, 0) else block(h, i, j, kind)
        c = pltpu.make_async_remote_copy(
            src_ref=src,
            dst_ref=block(h, i, j, kind),
            send_sem=ps.at[h, number(h, i, j), w],
            recv_sem=pr.at[h, number(h, i, j), w],
            device_id=(me, mate),
            device_id_type=MESH,
        )
        c.start()
        mates.setdefault(number(h, i, j), []).append(c)

    def got(h, i, j, kind=None):
        recvs[h, i, j, kind].wait_recv()

    both = (0, 1)
    local = []
    for h in both:
        c = pltpu.make_async_copy(own_ref.at[h], blocks[0].at[h, core], lsem.at[h])
        c.start()
        local.append(c)
    for h in both:
        for k in (1, 3):
            send(h, 0, 0, True, k)
    for h in both:
        to_mate(h, 0, 0)
        for k in (1, 3):
            send(h, 0, 0, False, k)

    def step_1():
        for h in both:
            for i, k, kind in ((3, 1, 0), (1, 3, 1)):
                got(h, i, 0)
                send(h, i, 0, True, k, kind)
                to_mate(h, i, 0)
        for h in both:
            for i in (3, 1):
                for k in (1, 3):
                    send(h, i, 0, False, k)

    def along_second(i):
        for h in both:
            for j, k, kind in ((3, 1, 0), (1, 3, 1)):
                got(h, i, j)
                send(h, i, j, False, k, kind)
                to_mate(h, i, j)

    def far_first():
        for h in both:
            for kind in (0, 1):
                got(h, 2, 0, kind)
                to_mate(h, 2, 0, kind)
            for k in (1, 3):
                send(h, 2, 0, False, k)

    def far_second(i):
        for h in both:
            for kind in (0, 1):
                got(h, i, 2, kind)
                to_mate(h, i, 2, kind)

    for r in range(16) if with_compute else ():
        rows = jnp.concatenate([q_ref[r, :, g * HD : (g + 1) * HD] for g in range(8)], axis=0)
        q_cols[r] = rows.T
    acc[...] = jnp.zeros_like(acc)
    acc_max[...] = jnp.full_like(acc_max, FLOOR_SCORE)
    v_cols[...] = jnp.ones_like(v_cols)

    def compute(dx, dz):
        n = dx * SIDE + dz
        if n == 0:
            for c in local:
                c.wait()
        for c in mates[n]:
            c.wait()
        if not with_compute:
            return
        ref = blocks[n]
        holder = lax.rem(place[0] + dx, SIDE) * SIDE + lax.rem(place[1] + dz, SIDE)
        for m in range(2):
            for half in range(2):
                v_cols[m, half * 64 : (half + 1) * 64, :] = ref[m, half, 1]
            k_rows[m] = jnp.concatenate([ref[m, 0, 0], ref[m, 1, 0]], axis=0).T

        def one_tile(i, _):
            request = tile_ref[holder * 12 + i]
            node = tile_ref[holder * 12 + 6 + i]
            score = jnp.dot(k_rows[node], q_cols[request], preferred_element_type=jnp.float32)
            top = jnp.max(score, axis=0, keepdims=True)
            weight = jnp.exp2(score * (SCALE * LOG2E) - top * (SCALE * LOG2E)).astype(jnp.bfloat16)
            mixed = jnp.dot(v_cols[node], weight, preferred_element_type=jnp.float32)
            part[i] = mixed[: HD + 8]
            part_max[i] = jnp.broadcast_to(top * SCALE, (8, 256))
            return 0

        lax.fori_loop(0, 6, one_tile, 0)

        def one_request(r, _):
            slot = slot_ref[holder * 32 + r]
            named = slot_ref[holder * 32 + 16 + r]
            here = named > 0
            new = jnp.where(here, part_max[slot], FLOOR_SCORE)
            old = acc_max[r]
            top = jnp.maximum(old, new)
            keep = jnp.exp(old - top)[:1]
            add = jnp.where(here, jnp.exp(new - top), 0.0)[:1]
            acc[r] = acc[r] * keep + part[slot] * add
            acc_max[r] = top
            return 0

        lax.fori_loop(0, 16, one_request, 0)

    step_1()
    compute(0, 0)
    along_second(0)
    compute(1, 0)
    far_first()
    compute(3, 0)
    compute(0, 1)
    along_second(3)
    along_second(1)
    compute(0, 3)
    far_second(0)
    compute(1, 1)
    along_second(2)
    compute(2, 0)
    compute(0, 2)
    far_second(3)
    far_second(1)
    far_second(2)
    for dx, dz in ((1, 3), (3, 1), (3, 3), (2, 1), (2, 3), (1, 2), (3, 2), (2, 2)):
        compute(dx, dz)
    for c in sends:
        c.wait_send()

    for r in range(16) if with_compute else ():
        total = acc[r, HD : HD + 1]
        some = total > 0.0
        inverse = jnp.where(some, 1.0 / jnp.where(some, total, 1.0), 0.0)
        rows = (acc[r, :HD] * inverse).T.astype(jnp.bfloat16)
        for g in range(8):
            o_ref[r, :, g * HD : (g + 1) * HD] = rows[g * 32 : (g + 1) * 32]
        level = acc_max[r, :1] + jnp.log(jnp.where(some, total, 1.0))
        lse_ref[r] = jnp.broadcast_to(jnp.where(some, level, FLOOR_SCORE), (8, 256))
    if not with_compute:
        o_ref[...] = q_ref[...]
        lse_ref[...] = jnp.zeros_like(lse_ref)


def run_tiles(tiles, slots, own, q, with_compute=True):
    vmem, smem = pl.BlockSpec(memory_space=pltpu.VMEM), pl.BlockSpec(memory_space=pltpu.SMEM)
    return pl.pallas_call(
        functools.partial(tiles_kernel, with_compute),
        out_shape=[jax.ShapeDtypeStruct((16, 32, 1024), jnp.bfloat16), jax.ShapeDtypeStruct((16, 8, 256), jnp.float32)],
        in_specs=[smem, smem, vmem, vmem],
        out_specs=[vmem, vmem],
        scratch_shapes=[
            *[pltpu.VMEM((2, 2, 2, 64, 1024), jnp.bfloat16) for _ in range(16)],
            pltpu.VMEM((16, HD, 256), jnp.bfloat16),
            pltpu.VMEM((2, 1024, HD), jnp.bfloat16),
            pltpu.VMEM((2, HD + 16, 1024), jnp.bfloat16),
            pltpu.VMEM((6, HD + 8, 256), jnp.float32),
            pltpu.VMEM((6, 8, 256), jnp.float32),
            pltpu.VMEM((16, HD + 8, 256), jnp.float32),
            pltpu.VMEM((16, 8, 256), jnp.float32),
            *[pltpu.SemaphoreType.DMA((2, 16, 2)) for _ in range(4)],
            pltpu.SemaphoreType.DMA((2,)),
        ],
        compiler_params=pltpu.CompilerParams(collective_id=3, has_side_effects=True, vmem_limit_bytes=48 * MIB),
    )(tiles, slots, own, q)


def merge_kernel(len_ref, q_ref, k_ref, v_ref, far_ref, lse_ref, o_ref):
    count = len_ref[0]
    rows = lax.broadcasted_iota(jnp.int32, (512, 512), 0)
    cols = lax.broadcasted_iota(jnp.int32, (512, 512), 1)
    allowed = (cols <= rows) & (cols < count)
    valid = rows[:, :1] < count
    for h in range(8):
        lanes = slice(h * HD, (h + 1) * HD)
        score = (
            lax.dot_general(q_ref[:, lanes], k_ref[...], (((1,), (1,)), ((), ())), preferred_element_type=jnp.float32) * SCALE
        )
        score = jnp.where(allowed, score, FLOOR_SCORE)
        top = jnp.max(score, axis=1, keepdims=True)
        weight = jnp.exp(score - top)
        total = jnp.sum(weight, axis=1, keepdims=True)
        mixed = jnp.dot(weight.astype(jnp.bfloat16), v_ref[...], preferred_element_type=jnp.float32)
        level = lse_ref[:, h : h + 1]
        peak = jnp.maximum(top, level)
        keep, add = jnp.exp(top - peak), jnp.exp(level - peak)
        far = far_ref[:, lanes].astype(jnp.float32)
        result = (mixed * keep + far * add) / (total * keep + add)
        o_ref[:, lanes] = jnp.where(valid, result, 0.0).astype(jnp.bfloat16)


def merge(count, q, k, v, far, level):
    vmem, smem = pl.BlockSpec(memory_space=pltpu.VMEM), pl.BlockSpec(memory_space=pltpu.SMEM)
    return pl.pallas_call(
        merge_kernel,
        out_shape=jax.ShapeDtypeStruct((512, 1024), jnp.bfloat16),
        in_specs=[smem] + [vmem] * 5,
        out_specs=vmem,
        compiler_params=pltpu.CompilerParams(vmem_limit_bytes=48 * MIB),
    )(count, q, k, v, far, level)


def body(queries, new_keys, new_values, key_cache, value_cache, page_owner, page_slot, tile_req, tile_node, suffix_len):
    dp_size = lax.axis_size("dp")
    dp_index = lax.axis_index("dp")
    parity = lax.axis_index("tensor") % 2
    owners = page_owner.reshape(dp_size, 16)
    slot_ids = page_slot.reshape(dp_size, 16)
    order = jnp.arange(16)
    same = owners[:, :, None] == owners[:, None, :]
    rank = jnp.sum(same & (order[None, :] < order[:, None])[None], axis=2)
    chosen = (owners[:, :, None] == dp_index) & (rank[:, :, None] == jnp.arange(CAP)[None, None, :])
    picked = jnp.sum(jnp.where(chosen, slot_ids[:, :, None], 0), axis=1)
    key_pages, value_pages = jnp.swapaxes(key_cache, 1, 2), jnp.swapaxes(value_cache, 1, 2)
    outgoing = jnp.stack([key_pages[picked], value_pages[picked]], axis=1)
    got = exchange(outgoing.reshape(4, 4, 512, 128), 0, 1).reshape(16, 2, CAP, 64, 128)
    my_owner = lax.dynamic_index_in_dim(owners, dp_index, 0, keepdims=False)
    my_rank = lax.dynamic_index_in_dim(rank, dp_index, 0, keepdims=False)
    rows = got[my_owner, :, my_rank].reshape(2, 8, 2, 64, 128)
    own = jnp.transpose(rows, (0, 2, 3, 1, 4)).reshape(2, 2, 64, 1024)

    spread = exchange(queries.reshape(4, 4, 32, 1024), 1, 2).reshape(16, 32, 1024)
    requests = tile_req.reshape(dp_size, 6)
    nodes = tile_node.reshape(dp_size, 6) - 2 * jnp.arange(dp_size, dtype=jnp.int32)[:, None]
    tiles = jnp.concatenate([requests, nodes], axis=1).reshape(-1)
    hits = requests[:, None, :] == jnp.arange(16)[None, :, None]
    slots = jnp.sum(jnp.where(hits, jnp.arange(6)[None, None, :], 0), axis=2)
    named = jnp.any(hits, axis=2)
    slots = jnp.concatenate([slots.astype(jnp.int32), named.astype(jnp.int32)], axis=1).reshape(-1)
    tile_out, tile_lse = run_tiles(tiles, slots, own, spread)

    far, level = exchange(tile_out.reshape(4, 4, 32, 1024), 1, 4, tile_lse)
    level = level[:, 0, :].reshape(16, 8, 32).transpose(0, 2, 1).reshape(512, 8)

    def join(block):
        other = from_partner(block)
        return jnp.concatenate([jnp.where(parity == 0, block, other), jnp.where(parity == 0, other, block)], axis=-1)

    keys, values = join(new_keys[0]), join(new_values[0])
    return merge(suffix_len, queries[0], keys, values, far.reshape(512, 1024), level)[None]


def solution(mesh):
    cut = P("dp", None, "tensor")
    return jax.shard_map(
        body,
        mesh=mesh,
        in_specs=(cut, cut, cut, cut, cut, P(), P(), P(), P(), P("dp")),
        out_specs=cut,
        check_vma=False,
    )
```

time: 858 us -> 210 us (0.24)
  waiting for transfers between devices: 313 us -> 0.01 us
  Pallas kernels: 0 us -> 192 us
  loops' own time: 142 us -> 0 us
  local copies, waits for them, and re-layouts: 148 us -> 14.5 us
  other arithmetic: 110 us -> 2.51 us
  matrix products: 68.5 us -> 0 us
  blocking collectives: 33.4 us -> 0 us
  starting transfers between devices: 22.4 us -> 0.58 us
  between operations: 14.4 us -> 0.87 us
    all_to_all x4 -> x0, waiting for transfers between devices: 246 us -> none  [the longest x1 227 us: body(): lax.all_to_all(out_buffer, 'dp', split_axis=0, concat_axis=0, tiled=True)]
    pallas_call x0 -> x5, Pallas kernels: none -> 192 us  [the longest x1 110 us: run_tiles(): pl.pallas_call(functools.partial(tiles_kernel, with_compute), out_shape=[...]
    another operation x9 -> x0, loops' own time: 142 us -> none  [the longest x7 107 us: head_loop(): row_max, row_sum, mixed = lax.map(one_head, jnp.arange(query_rows.shape[1]))]
    dot_general x112 -> x0, matrix products: 68.5 us -> none  [the longest x56 36.9 us: softmax_part(): lax.dot_general(query_rows, key_rows, (((1,), (1,)), ((), ())), preferred...]
    all_gather x1 -> x0, waiting for transfers between devices: 64.7 us -> none  [body(): everyone = lax.all_gather(queries, 'dp', axis=0, tiled=True)]
    dynamic_slice x118 -> x0, local copies, waits for them, and re-layouts: 58.3 us -> none  [the longest x56 33.9 us: head_loop(): row_max, row_sum, mixed = lax.map(one_head, jnp.arange(query_rows.shape[1]))]
    add x17 -> x0, other arithmetic: 47.8 us -> none  [the longest x16 47.1 us: add_holder(): return running + holder_rows * far_factor[holder_index][..., None]]
    all_to_all x1 -> x0, blocking collectives: 33.4 us -> none  [body(): lax.all_to_all(send_values, 'dp', split_axis=0, concat_axis=0, tiled=True)]
  transfers between devices with their start and end apart: 9 -> 2, of which waited for: 5 -> 0; matrix products, arithmetic and copies ran while one was open for 10% -> 6% of each run, Pallas kernels for 0% -> 87%
where the time goes in v1:
time: 210 us
  Pallas kernels  192 us (91%)
  local copies, waits for them, and re-layouts  14.5 us (7%)
  other arithmetic  2.51 us (1%)
    pallas_call x1, Pallas kernels, run_tiles(): pl.pallas_call(functools.partial(tiles_kernel, with_compute), out_shape=[...  110 us
    pallas_call x3, Pallas kernels, exchange(): pl.pallas_call(functools.partial(exchange_kernel, axis, small is not None...  73.2 us
    pallas_call x1, Pallas kernels, merge(): pl.pallas_call(merge_kernel, out_shape=jax.ShapeDtypeStruct((512, 1024),...  8.27 us
    unnamed x10, local copies, waits for them, and re-layouts  5.53 us
  transfers between devices with their start and end apart: 2, of which 0 were waited for; matrix products, arithmetic and copies ran while one was open for 6% of the time, Pallas kernels for 87%

profile of v1, /device:TPU:0, one launch (start us, length us, event | category | flops | bytes accessed | tf_op | source)
XLA Modules:
  0.0 210.1 jit_solution(17826144948708164335)
XLA Ops:
  0.0 1.0 copy.27
  1.1 1.6 copy.26
  2.7 0.5 collective-permute-start
  3.3 0.7 reshape.138
  5.1 0.7 reshape.139
  6.1 0.8 copy.29
  6.9 0.4 convert_reduce_fusion
  7.4 0.8 copy.30
  8.2 0.1 select_reduce_fusion.1
  8.6 0.7 gather_fusion.1
  9.3 2.0 gather_fusion
  11.3 0.2 pad_maximum_fusion
  11.5 31.5 %shard_map.100 = bf16[4,4,512,128]{3,2,1,0:T(8,128)(2,1)S(1)} custom-call(bf16[4,4,512,128]{3,2,1,0:T(8,128)(2,1)S(1)} %bitcast.49), custom_call_target="tpu_custom_call" | custom-call | tf_op jit(solution)/shard_map/pallas_call | solution.py:141
  43.0 1.3 copy-done.2
  44.4 2.3 %gather_fusion.2 = bf16[16,2,64,128]{3,2,1,0:T(8,128)(2,1)S(1)} fusion(bf16[16,2,4,64,128]{4,3,2,1,0:T(8,128)(2,1)} %bitcast.53, s32[16]{0:T(128)S(1)} %fusion.7), kind=kCustom, calls=%fused_computation.2 | custom fusion | bytes 1048704 | tf_op jit(solution)/shard_map/gather | solution.py:419
  46.7 0.1 copy.38
  46.9 19.7 %shard_map.101 = bf16[4,4,32,1024]{3,2,1,0:T(8,128)(2,1)S(1)} custom-call(bf16[4,4,32,1024]{3,2,1,0:T(8,128)(2,1)S(1)} %bitcast.51), custom_call_target="tpu_custom_call" | custom-call | tf_op jit(solution)/shard_map/pallas_call | solution.py:141
  66.5 110.2 %shard_map.102 = (bf16[16,32,1024]{2,1,0:T(8,128)(2,1)S(1)}, f32[16,8,256]{2,1,0:T(8,128)S(1)}) custom-call(s32[192]{0:T(256)S(1)} %reshape.140.tile_ref, s32[512]{0:T(512)S(1)} %reshape.141.slot_ref, bf16[2,2,64,1024]{3,2,1,0:T(8,128)(2,1)S(1)} %bitcast.54, bf16[16,32,1024]{2,1,0:T(8,128)(2,1)S(1)} %bitcast.50), custom_call_target="tpu_custom_call" | custom-call | tf_op jit(solution)/shard_map/pallas_call | solution.py:347
  176.8 22.0 %shard_map.103 = (bf16[4,4,32,1024]{3,2,1,0:T(8,128)(2,1)S(1)}, f32[16,8,256]{2,1,0:T(8,128)S(1)}) custom-call(bf16[4,4,32,1024]{3,2,1,0:T(8,128)(2,1)S(1)} %bitcast.55, f32[16,8,256]{2,1,0:T(8,128)S(1)} %get-tuple-element.10.refs_1_), custom_call_target="tpu_custom_call" | custom-call | tf_op jit(solution)/shard_map/pallas_call | solution.py:141
  198.8 0.7 reshape_squeeze.3
  199.5 1.0 copy.35
  200.5 1.1 broadcast_select_fusion.1
  201.6 0.1 pad_maximum_fusion.2.v_ref
  201.8 8.3 %shard_map.104 = bf16[512,1024]{1,0:T(8,128)(2,1)} custom-call(s32[1]{0:T(128)S(6)} %copy.39.len_ref, bf16[512,1024]{1,0:T(8,128)(2,1)S(1)} %bitcast.52, bf16[512,128]{1,0:T(8,128)(2,1)S(1)} %pad_maximum_fusion.1.k_ref, bf16[512,128]{1,0:T(8,128)(2,1)S(1)} %pad_maximum_fusion.2.v_ref, bf16[512,1024]{1,0:T(8,128)(2,1)S(1)} %bitcast.56, f32[512,8]{1,0:T(8,128)S(1)} %bitcast.57), custom_call_target="tpu_custom_call" | custom-call | tf_op jit(solution)/shard_map/pallas_call | solution.py:394
  (29 shorter events, 1.3 us)
Async XLA Ops:
  0.0 8.6 %copy-start = (bf16[64,128,64]{1,2,0:T(8,128)(2,1)S(1)}, bf16[64,128,64]{1,2,0:T(8,128)(2,1)}, u32[]{:S(2)}) copy-start(bf16[64,128,64]{1,2,0:T(8,128)(2,1)} %param.14) | copy-start | bytes 3145732
  1.1 199.5 %collective-permute-start.1 = (bf16[512,64]{1,0:T(8,128)(2,1)S(1)}, bf16[512,64]{1,0:T(8,128)(2,1)}, u32[]{:S(2)}, u32[]{:S(2)}) collective-permute-start(bf16[512,64]{1,0:T(8,128)(2,1)S(1)} %bitcast.62), channel_id=1, source_target_pairs={{0,1},{1,0},{2,3},{3,2},{4,5},{5,4},{6,7},{7,6},{8,9},{9,8},{10,11... | collective-permute-start | bytes 196616 | tf_op jit(solution)/shard_map/ppermute | solution.py:22
  2.7 197.8 %collective-permute-start = (bf16[512,64]{1,0:T(8,128)(2,1)}, bf16[512,64]{1,0:T(8,128)(2,1)}, u32[]{:S(2)}, u32[]{:S(2)}) collective-permute-start(bf16[512,64]{1,0:T(8,128)(2,1)} %bitcast.1), channel_id=1, source_target_pairs={{0,1},{1,0},{2,3},{3,2},{4,5},{5,4},{6,7},{7,6},{8,9},{9,8},{10,11... | collective-permute-start | bytes 196616 | tf_op jit(solution)/shard_map/ppermute | solution.py:22
  43.0 1.4 copy-start.2
  44.4 2.5 %copy-start.1 = (bf16[1,512,1024]{2,1,0:T(8,128)(2,1)S(1)}, bf16[1,512,1024]{2,1,0:T(8,128)(2,1)}, u32[]{:S(2)}) copy-start(bf16[1,512,1024]{2,1,0:T(8,128)(2,1)} %param.10) | copy-start | bytes 3145732

commit v2 on v1

--- a/solution.py
+++ b/solution.py
@@ -149,18 +149,31 @@
     return out[0] if small is None else out
 
 
-def tiles_kernel(with_compute, tile_ref, slot_ref, own_ref, q_ref, o_ref, lse_ref, *scratch):
-    blocks = scratch[:16]
-    q_cols, k_rows, v_cols, part, part_max, acc, acc_max, ss, rs, ps, pr, lsem = scratch[16:]
+ORDER = (
+    (0, 0), (1, 0), (3, 0), (0, 1), (0, 3), (2, 0), (0, 2), (1, 1),
+    (1, 3), (3, 1), (3, 3), (2, 1), (2, 3), (1, 2), (3, 2), (2, 2),
+)
+
+
+def pick(index, values):
+    out = jnp.int32(values[0])
+    for i, v in enumerate(values[1:], 1):
+        out = jnp.where(index == i, jnp.int32(v), out)
+    return out
+
+
+def tiles_kernel(tile_ref, slot_ref, own_ref, q_ref, o_ref, lse_ref, *scratch):
+    blocks, q_cols, k_rows, v_cols, part, part_max, acc, acc_max, ss, rs, ps, pr, lsem = scratch
     me, t = lax.axis_index("dp"), lax.axis_index("tensor")
     core = lax.rem(t, 2)
     mate = t + 1 - 2 * core
     place = (me // SIDE, me % SIDE)
+    beside = {(a, k): neighbour(me, a, k) for a in (0, 1) for k in (1, 3)}
 
     barrier = pltpu.get_barrier_semaphore()
     for a in (0, 1):
         for k in (1, 3):
-            pl.semaphore_signal(barrier, inc=1, device_id=(neighbour(me, a, k), t), device_id_type=MESH)
+            pl.semaphore_signal(barrier, inc=1, device_id=(beside[a, k], t), device_id_type=MESH)
     pl.semaphore_signal(barrier, inc=1, device_id=(me, mate), device_id_type=MESH)
     pl.semaphore_wait(barrier, 5)
 
@@ -169,166 +182,181 @@
         return i * SIDE + j if h == 0 else j * SIDE + i
 
     def block(h, i, j, kind):
-        ref = blocks[number(h, i, j)].at[h, core]
+        ref = blocks.at[number(h, i, j), h, core]
         return ref if kind is None else ref.at[kind]
 
-    sends, recvs, mates = [], {}, {}
-
-    def send(h, i, j, first, k, kind=None):
+    def origin(h, i, j, kind):
+        return own_ref.at[h] if (i, j) == (0, 0) else block(h, i, j, kind)
+
+    def hop(h, i, j, first, k, kind, group):
         to = (i - k, j) if first else (i, j - k)
-        a = h if first else 1 - h
-        w = 0 if kind is None else kind
-        src = own_ref.at[h] if (i, j) == (0, 0) else block(h, i, j, kind)
-        c = pltpu.make_async_remote_copy(
-            src_ref=src,
+        pltpu.make_async_remote_copy(
+            src_ref=origin(h, i, j, kind),
             dst_ref=block(h, *to, kind),
-            send_sem=ss.at[h, number(h, *to), w],
-            recv_sem=rs.at[h, number(h, *to), w],
-            device_id=(neighbour(me, a, k), t),
+            send_sem=ss.at[0],
+            recv_sem=rs.at[group],
+            device_id=(beside[h if first else 1 - h, k], t),
             device_id_type=MESH,
-        )
-        c.start()
-        sends.append(c)
-        recvs[h, to[0] % SIDE, to[1] % SIDE, kind] = c
-
-    def to_mate(h, i, j, kind=None):
-        w = 0 if kind is None else kind
-        src = own_ref.at[h] if (i, j) == (0, 0) else block(h, i, j, kind)
-        c = pltpu.make_async_remote_copy(
-            src_ref=src,
-            dst_ref=block(h, i, j, kind),
-            send_sem=ps.at[h, number(h, i, j), w],
-            recv_sem=pr.at[h, number(h, i, j), w],
+        ).start()
+
+    def taken(sem, holders_of_two):
+        like = blocks.at[pl.ds(0, holders_of_two), :, 0]
+        pltpu.make_async_copy(like, like, sem).wait()
+
+    def across(n):
+        return pltpu.make_async_remote_copy(
+            src_ref=blocks.at[n, :, core],
+            dst_ref=blocks.at[n, :, core],
+            send_sem=ps.at[n],
+            recv_sem=pr.at[n],
             device_id=(me, mate),
             device_id_type=MESH,
         )
-        c.start()
-        mates.setdefault(number(h, i, j), []).append(c)
-
-    def got(h, i, j, kind=None):
-        recvs[h, i, j, kind].wait_recv()
+
+    def to_mate(*holders_here):
+        for dx, dz in holders_here:
+            across(dx * SIDE + dz).start()
 
     both = (0, 1)
     local = []
     for h in both:
-        c = pltpu.make_async_copy(own_ref.at[h], blocks[0].at[h, core], lsem.at[h])
+        c = pltpu.make_async_copy(own_ref.at[h], blocks.at[0, h, core], lsem.at[h])
         c.start()
         local.append(c)
     for h in both:
         for k in (1, 3):
-            send(h, 0, 0, True, k)
+            hop(h, 0, 0, True, k, None, 0)
     for h in both:
-        to_mate(h, 0, 0)
         for k in (1, 3):
-            send(h, 0, 0, False, k)
-
-    def step_1():
+            hop(h, 0, 0, False, k, None, 1)
+
+    def near_first():
+        taken(rs.at[0], 2)
         for h in both:
-            for i, k, kind in ((3, 1, 0), (1, 3, 1)):
-                got(h, i, 0)
-                send(h, i, 0, True, k, kind)
-                to_mate(h, i, 0)
+            hop(h, 3, 0, True, 1, 0, 2)
+            hop(h, 1, 0, True, 3, 1, 2)
+
+    def near_second(i, group):
+        for h in both:
+            hop(h, i, 3, False, 1, 0, group)
+            hop(h, i, 1, False, 3, 1, group)
+
+    def own_second():
+        taken(rs.at[1], 2)
+        near_second(0, 3)
+
+    def near_on():
         for h in both:
             for i in (3, 1):
                 for k in (1, 3):
-                    send(h, i, 0, False, k)
-
-    def along_second(i):
+                    hop(h, i, 0, False, k, None, 4)
+
+    def far_first():
+        taken(rs.at[2], 1)
         for h in both:
-            for j, k, kind in ((3, 1, 0), (1, 3, 1)):
-                got(h, i, j)
-                send(h, i, j, False, k, kind)
-                to_mate(h, i, j)
-
-    def far_first():
-        for h in both:
-            for kind in (0, 1):
-                got(h, 2, 0, kind)
-                to_mate(h, 2, 0, kind)
             for k in (1, 3):
-                send(h, 2, 0, False, k)
-
-    def far_second(i):
-        for h in both:
-            for kind in (0, 1):
-                got(h, i, 2, kind)
-                to_mate(h, i, 2, kind)
-
-    for r in range(16) if with_compute else ():
+                hop(h, 2, 0, False, k, None, 6)
+
+    def far_own():
+        taken(rs.at[3], 1)
+        to_mate((2, 0), (0, 2))
+
+    def near_near():
+        taken(rs.at[4], 4)
+        for i in (3, 1):
+            near_second(i, 5)
+        to_mate((1, 1), (1, 3), (3, 1), (3, 3))
+
+    def far_near():
+        taken(rs.at[6], 2)
+        near_second(2, 7)
+
+    def near_far():
+        taken(rs.at[5], 2)
+        to_mate((2, 1), (2, 3), (1, 2), (3, 2))
+
+    def far_far():
+        taken(rs.at[7], 1)
+        to_mate((2, 2))
+
+    def arrived(dx, dz):
+        across(dx * SIDE + dz).wait()
+
+    numbers = [dx * SIDE + dz for dx, dz in ORDER]
+    holders = [lax.rem(place[0] + dx, SIDE) * SIDE + lax.rem(place[1] + dz, SIDE) for dx, dz in ORDER]
+
+    def prepare(n, buf):
+        for m in range(2):
+            for half in range(2):
+                v_cols[buf, m, half * 64 : (half + 1) * 64, :] = blocks[n, m, half, 1]
+            k_rows[buf, m] = jnp.concatenate([blocks[n, m, 0, 0], blocks[n, m, 1, 0]], axis=0).T
+
+    def compute(holder, buf):
+        nodes = [tile_ref[holder * 12 + 6 + i] for i in range(6)]
+        scores = [
+            jnp.dot(k_rows[buf, nodes[i]], q_cols[tile_ref[holder * 12 + i]], preferred_element_type=jnp.float32)
+            for i in range(6)
+        ]
+        for i in range(6):
+            top = jnp.max(scores[i], axis=0, keepdims=True)
+            weight = jnp.exp2(scores[i] * (SCALE * LOG2E) - top * (SCALE * LOG2E)).astype(jnp.bfloat16)
+            mixed = jnp.dot(v_cols[buf, nodes[i]], weight, preferred_element_type=jnp.float32)
+            part[buf, i] = mixed[: HD + 8]
+            part_max[buf, i] = jnp.broadcast_to(top * SCALE, (8, 256))
+
+    def combine(holder, buf):
+        for r in range(16):
+            slot = slot_ref[holder * 32 + r]
+            here = slot_ref[holder * 32 + 16 + r] > 0
+            new = jnp.where(here, part_max[buf, slot], FLOOR_SCORE)
+            old = acc_max[r]
+            top = jnp.maximum(old, new)
+            keep = jnp.exp(old - top)[:1]
+            add = jnp.where(here, jnp.exp(new - top), 0.0)[:1]
+            acc[r] = acc[r] * keep + part[buf, slot] * add
+            acc_max[r] = top
+
+    for r in range(16):
         rows = jnp.concatenate([q_ref[r, :, g * HD : (g + 1) * HD] for g in range(8)], axis=0)
         q_cols[r] = rows.T
     acc[...] = jnp.zeros_like(acc)
     acc_max[...] = jnp.full_like(acc_max, FLOOR_SCORE)
     v_cols[...] = jnp.ones_like(v_cols)
 
-    def compute(dx, dz):
-        n = dx * SIDE + dz
-        if n == 0:
-            for c in local:
-                c.wait()
-        for c in mates[n]:
-            c.wait()
-        if not with_compute:
-            return
-        ref = blocks[n]
-        holder = lax.rem(place[0] + dx, SIDE) * SIDE + lax.rem(place[1] + dz, SIDE)
-        for m in range(2):
-            for half in range(2):
-                v_cols[m, half * 64 : (half + 1) * 64, :] = ref[m, half, 1]
-            k_rows[m] = jnp.concatenate([ref[m, 0, 0], ref[m, 1, 0]], axis=0).T
-
-        def one_tile(i, _):
-            request = tile_ref[holder * 12 + i]
-            node = tile_ref[holder * 12 + 6 + i]
-            score = jnp.dot(k_rows[node], q_cols[request], preferred_element_type=jnp.float32)
-            top = jnp.max(score, axis=0, keepdims=True)
-            weight = jnp.exp2(score * (SCALE * LOG2E) - top * (SCALE * LOG2E)).astype(jnp.bfloat16)
-            mixed = jnp.dot(v_cols[node], weight, preferred_element_type=jnp.float32)
-            part[i] = mixed[: HD + 8]
-            part_max[i] = jnp.broadcast_to(top * SCALE, (8, 256))
-            return 0
-
-        lax.fori_loop(0, 6, one_tile, 0)
-
-        def one_request(r, _):
-            slot = slot_ref[holder * 32 + r]
-            named = slot_ref[holder * 32 + 16 + r]
-            here = named > 0
-            new = jnp.where(here, part_max[slot], FLOOR_SCORE)
-            old = acc_max[r]
-            top = jnp.maximum(old, new)
-            keep = jnp.exp(old - top)[:1]
-            add = jnp.where(here, jnp.exp(new - top), 0.0)[:1]
-            acc[r] = acc[r] * keep + part[slot] * add
-            acc_max[r] = top
-            return 0
-
-        lax.fori_loop(0, 16, one_request, 0)
-
-    step_1()
-    compute(0, 0)
-    along_second(0)
-    compute(1, 0)
-    far_first()
-    compute(3, 0)
-    compute(0, 1)
-    along_second(3)
-    along_second(1)
-    compute(0, 3)
-    far_second(0)
-    compute(1, 1)
-    along_second(2)
-    compute(2, 0)
-    compute(0, 2)
-    far_second(3)
-    far_second(1)
-    far_second(2)
-    for dx, dz in ((1, 3), (3, 1), (3, 3), (2, 1), (2, 3), (1, 2), (3, 2), (2, 2)):
-        compute(dx, dz)
-    for c in sends:
-        c.wait_send()
-
-    for r in range(16) if with_compute else ():
+    for c in local:
+        c.wait()
+    to_mate((0, 0))
+    arrived(0, 0)
+    prepare(0, 0)
+    compute(holders[0], 0)
+    near_first()
+    own_second()
+    near_on()
+    to_mate((1, 0), (3, 0), (0, 1), (0, 3))
+    arrived(*ORDER[1])
+    prepare(numbers[1], 1)
+    events = {1: far_first, 3: far_own, 5: near_near, 8: far_near, 9: near_far, 12: far_far}
+
+    def step(at, _):
+        for i in range(1, 15):
+
+            @pl.when(at == i)
+            def _(i=i):
+                if i in events:
+                    events[i]()
+                arrived(*ORDER[i + 1])
+
+        buf = at % 2
+        combine(pick(at - 1, holders), 1 - buf)
+        compute(pick(at, holders), buf)
+        prepare(pick(at + 1, numbers + numbers[-1:]), 1 - buf)
+        return 0
+
+    lax.fori_loop(1, 16, step, 0)
+    combine(holders[15], 1)
+    taken(ss.at[0], 15)
+
+    for r in range(16):
         total = acc[r, HD : HD + 1]
         some = total > 0.0
         inverse = jnp.where(some, 1.0 / jnp.where(some, total, 1.0), 0.0)
@@ -337,28 +365,28 @@
             o_ref[r, :, g * HD : (g + 1) * HD] = rows[g * 32 : (g + 1) * 32]
         level = acc_max[r, :1] + jnp.log(jnp.where(some, total, 1.0))
         lse_ref[r] = jnp.broadcast_to(jnp.where(some, level, FLOOR_SCORE), (8, 256))
-    if not with_compute:
-        o_ref[...] = q_ref[...]
-        lse_ref[...] = jnp.zeros_like(lse_ref)
-
-
-def run_tiles(tiles, slots, own, q, with_compute=True):
+
+
+def run_tiles(tiles, slots, own, q):
     vmem, smem = pl.BlockSpec(memory_space=pltpu.VMEM), pl.BlockSpec(memory_space=pltpu.SMEM)
     return pl.pallas_call(
-        functools.partial(tiles_kernel, with_compute),
+        tiles_kernel,
         out_shape=[jax.ShapeDtypeStruct((16, 32, 1024), jnp.bfloat16), jax.ShapeDtypeStruct((16, 8, 256), jnp.float32)],
         in_specs=[smem, smem, vmem, vmem],
         out_specs=[vmem, vmem],
         scratch_shapes=[
-            *[pltpu.VMEM((2, 2, 2, 64, 1024), jnp.bfloat16) for _ in range(16)],
+            pltpu.VMEM((16, 2, 2, 2, 64, 1024), jnp.bfloat16),
             pltpu.VMEM((16, HD, 256), jnp.bfloat16),
-            pltpu.VMEM((2, 1024, HD), jnp.bfloat16),
-            pltpu.VMEM((2, HD + 16, 1024), jnp.bfloat16),
-            pltpu.VMEM((6, HD + 8, 256), jnp.float32),
-            pltpu.VMEM((6, 8, 256), jnp.float32),
+            pltpu.VMEM((2, 2, 1024, HD), jnp.bfloat16),
+            pltpu.VMEM((2, 2, HD + 16, 1024), jnp.bfloat16),
+            pltpu.VMEM((2, 6, HD + 8, 256), jnp.float32),
+            pltpu.VMEM((2, 6, 8, 256), jnp.float32),
             pltpu.VMEM((16, HD + 8, 256), jnp.float32),
             pltpu.VMEM((16, 8, 256), jnp.float32),
-            *[pltpu.SemaphoreType.DMA((2, 16, 2)) for _ in range(4)],
+            pltpu.SemaphoreType.DMA((1,)),
+            pltpu.SemaphoreType.DMA((8,)),
+            pltpu.SemaphoreType.DMA((16,)),
+            pltpu.SemaphoreType.DMA((16,)),
             pltpu.SemaphoreType.DMA((2,)),
         ],
         compiler_params=pltpu.CompilerParams(collective_id=3, has_side_effects=True, vmem_limit_bytes=48 * MIB),

time: 210 us -> 167 us (0.80)
  Pallas kernels: 192 us -> 148 us
    pallas_call x1, Pallas kernels: 110 us -> 66.7 us  [run_tiles(): pl.pallas_call(tiles_kernel, out_shape=[jax.ShapeDtypeStruct((16, 32, 102...]
  transfers between devices with their start and end apart: 2 -> 2, of which waited for: 0 -> 0; matrix products, arithmetic and copies ran while one was open for 6% -> 8% of each run, Pallas kernels for 87% -> 84%
where the time goes in v2:
time: 167 us
  Pallas kernels  148 us (89%)
  local copies, waits for them, and re-layouts  14.5 us (9%)
  other arithmetic  2.51 us (2%)
    pallas_call x3, Pallas kernels, exchange(): pl.pallas_call(functools.partial(exchange_kernel, axis, small is not None...  73.1 us
    pallas_call x1, Pallas kernels, run_tiles(): pl.pallas_call(tiles_kernel, out_shape=[jax.ShapeDtypeStruct((16, 32, 102...  66.7 us
    pallas_call x1, Pallas kernels, merge(): pl.pallas_call(merge_kernel, out_shape=jax.ShapeDtypeStruct((512, 1024),...  8.27 us
    unnamed x10, local copies, waits for them, and re-layouts  5.53 us
  transfers between devices with their start and end apart: 2, of which 0 were waited for; matrix products, arithmetic and copies ran while one was open for 8% of the time, Pallas kernels for 84%

profile of v2, /device:TPU:0, one launch (start us, length us, event | category | flops | bytes accessed | tf_op | source)
XLA Modules:
  0.0 166.5 jit_solution(6561810553135473834)
XLA Ops:
  0.0 1.0 copy.27
  1.1 1.6 copy.26
  2.7 0.5 collective-permute-start
  3.3 0.7 reshape.138
  5.1 0.7 reshape.139
  6.1 0.8 copy.29
  6.9 0.4 convert_reduce_fusion
  7.4 0.8 copy.30
  8.2 0.1 select_reduce_fusion.1
  8.6 0.7 gather_fusion.1
  9.3 2.0 %gather_fusion = bf16[64,64,128]{2,1,0:T(8,128)(2,1)S(1)} fusion(bf16[64,64,128]{2,1,0:T(8,128)(2,1)} %bitcast.61, s32[1024]{0:T(1024)S(1)} %pad_clamp_fusion), kind=kCustom, calls=%fused_computation | custom fusion | bytes 2097408 | tf_op jit(solution)/shard_map/gather | solution.py:443
  11.3 0.2 pad_maximum_fusion
  11.5 31.5 %shard_map.100 = bf16[4,4,512,128]{3,2,1,0:T(8,128)(2,1)S(1)} custom-call(bf16[4,4,512,128]{3,2,1,0:T(8,128)(2,1)S(1)} %bitcast.49), custom_call_target="tpu_custom_call" | custom-call | tf_op jit(solution)/shard_map/pallas_call | solution.py:141
  43.0 1.3 copy-done.2
  44.4 2.3 %gather_fusion.2 = bf16[16,2,64,128]{3,2,1,0:T(8,128)(2,1)S(1)} fusion(bf16[16,2,4,64,128]{4,3,2,1,0:T(8,128)(2,1)} %bitcast.53, s32[16]{0:T(128)S(1)} %fusion.7), kind=kCustom, calls=%fused_computation.2 | custom fusion | bytes 1048704 | tf_op jit(solution)/shard_map/gather | solution.py:447
  46.7 0.1 copy.38
  46.9 19.7 %shard_map.101 = bf16[4,4,32,1024]{3,2,1,0:T(8,128)(2,1)S(1)} custom-call(bf16[4,4,32,1024]{3,2,1,0:T(8,128)(2,1)S(1)} %bitcast.51), custom_call_target="tpu_custom_call" | custom-call | tf_op jit(solution)/shard_map/pallas_call | solution.py:141
  66.5 66.7 %shard_map.102 = (bf16[16,32,1024]{2,1,0:T(8,128)(2,1)S(1)}, f32[16,8,256]{2,1,0:T(8,128)S(1)}) custom-call(s32[192]{0:T(256)S(1)} %reshape.140.tile_ref, s32[512]{0:T(512)S(1)} %reshape.141.slot_ref, bf16[2,2,64,1024]{3,2,1,0:T(8,128)(2,1)S(1)} %bitcast.54, bf16[16,32,1024]{2,1,0:T(8,128)(2,1)S(1)} %bitcast.50), custom_call_target="tpu_custom_call" | custom-call | tf_op jit(solution)/shard_map/pallas_call | solution.py:372
  133.3 21.9 %shard_map.103 = (bf16[4,4,32,1024]{3,2,1,0:T(8,128)(2,1)S(1)}, f32[16,8,256]{2,1,0:T(8,128)S(1)}) custom-call(bf16[4,4,32,1024]{3,2,1,0:T(8,128)(2,1)S(1)} %bitcast.55, f32[16,8,256]{2,1,0:T(8,128)S(1)} %get-tuple-element.10.refs_1_), custom_call_target="tpu_custom_call" | custom-call | tf_op jit(solution)/shard_map/pallas_call | solution.py:141
  155.2 0.7 reshape_squeeze.3
  155.9 1.0 copy.35
  156.9 1.1 broadcast_select_fusion.1
  158.0 0.1 pad_maximum_fusion.2.v_ref
  158.2 8.3 %shard_map.104 = bf16[512,1024]{1,0:T(8,128)(2,1)} custom-call(s32[1]{0:T(128)S(6)} %copy.39.len_ref, bf16[512,1024]{1,0:T(8,128)(2,1)S(1)} %bitcast.52, bf16[512,128]{1,0:T(8,128)(2,1)S(1)} %pad_maximum_fusion.1.k_ref, bf16[512,128]{1,0:T(8,128)(2,1)S(1)} %pad_maximum_fusion.2.v_ref, bf16[512,1024]{1,0:T(8,128)(2,1)S(1)} %bitcast.56, f32[512,8]{1,0:T(8,128)S(1)} %bitcast.57), custom_call_target="tpu_custom_call" | custom-call | tf_op jit(solution)/shard_map/pallas_call | solution.py:422
  (29 shorter events, 1.3 us)
Async XLA Ops:
  0.0 8.6 %copy-start = (bf16[64,128,64]{1,2,0:T(8,128)(2,1)S(1)}, bf16[64,128,64]{1,2,0:T(8,128)(2,1)}, u32[]{:S(2)}) copy-start(bf16[64,128,64]{1,2,0:T(8,128)(2,1)} %param.14) | copy-start | bytes 3145732
  1.1 155.9 %collective-permute-start.1 = (bf16[512,64]{1,0:T(8,128)(2,1)S(1)}, bf16[512,64]{1,0:T(8,128)(2,1)}, u32[]{:S(2)}, u32[]{:S(2)}) collective-permute-start(bf16[512,64]{1,0:T(8,128)(2,1)S(1)} %bitcast.62), channel_id=1, source_target_pairs={{0,1},{1,0},{2,3},{3,2},{4,5},{5,4},{6,7},{7,6},{8,9},{9,8},{10,11... | collective-permute-start | bytes 196616 | tf_op jit(solution)/shard_map/ppermute | solution.py:22
  2.7 154.2 %collective-permute-start = (bf16[512,64]{1,0:T(8,128)(2,1)}, bf16[512,64]{1,0:T(8,128)(2,1)}, u32[]{:S(2)}, u32[]{:S(2)}) collective-permute-start(bf16[512,64]{1,0:T(8,128)(2,1)} %bitcast.1), channel_id=1, source_target_pairs={{0,1},{1,0},{2,3},{3,2},{4,5},{5,4},{6,7},{7,6},{8,9},{9,8},{10,11... | collective-permute-start | bytes 196616 | tf_op jit(solution)/shard_map/ppermute | solution.py:22
  43.0 1.4 copy-start.2
  44.4 2.5 %copy-start.1 = (bf16[1,512,1024]{2,1,0:T(8,128)(2,1)S(1)}, bf16[1,512,1024]{2,1,0:T(8,128)(2,1)}, u32[]{:S(2)}) copy-start(bf16[1,512,1024]{2,1,0:T(8,128)(2,1)} %param.10) | copy-start | bytes 3145732

commit v3 on v2

v3 whole, which is shorter than its diff:
```python
import functools
import math

import jax
import jax.numpy as jnp
from jax import lax
from jax.experimental import pallas as pl
from jax.experimental.pallas import tpu as pltpu
from jax.sharding import PartitionSpec as P

HD = 128
CAP = 4
SIDE = 4
FLOOR_SCORE = -1e30
SCALE = 1.0 / math.sqrt(HD)
LOG2E = math.log2(math.e)
MESH = pl.DeviceIdType.MESH
MIB = 1 << 20


def neighbour(me, axis, step):
    slow, fast = me // SIDE, me % SIDE
    if axis == 0:
        return lax.rem(slow + step, SIDE) * SIDE + fast
    return slow * SIDE + lax.rem(fast + step, SIDE)


class Exchange:
    def __init__(self, me, tensor, x, out, mid, relay, sems, quarter, part):
        self.me, self.t, self.x, self.out, self.mid, self.relay = me, tensor, x, out, mid, relay
        self.s1, self.r1, self.s2, self.r2, self.local = sems
        self.place = (me // SIDE, me % SIDE)
        self.quarter, self.part = quarter, part

    def crd(self, a, k):
        return lax.rem(self.place[a] + k, SIDE)

    def copy(self, src, dst, ss, rs, a, k):
        c = pltpu.make_async_remote_copy(
            src_ref=src, dst_ref=dst, send_sem=ss, recv_sem=rs, device_id=(neighbour(self.me, a, k), self.t), device_id_type=MESH
        )
        c.start()
        return c

    def source(self, second, h, i, sub):
        if second:
            return self.part(self.mid.at[h, :, i], sub)
        return self.quarter(self.x.at[i] if h == 0 else self.x.at[:, i], h, sub)

    def target(self, second, h, i, sub):
        if second:
            return self.quarter(self.out.at[:, i] if h == 0 else self.out.at[i], h, sub)
        return self.part(self.mid.at[h, i], sub)

    def start(self, second):
        ss, rs = (self.s2, self.r2) if second else (self.s1, self.r1)
        self.far, self.near = [], []
        for h in (0, 1):
            a = 1 - h if second else h
            mine = self.crd(a, 0)
            for j, k in ((0, 1), (1, 3)):
                c = self.copy(
                    self.source(second, h, self.crd(a, 2), j), self.relay.at[int(second), h, j], ss.at[h, 0, j], rs.at[h, 0, j], a, k
                )
                self.far.append((h, j, k, a, c))
            for j, k in ((0, 1), (1, 3)):
                self.near.append(
                    self.copy(
                        self.source(second, h, self.crd(a, k), None), self.target(second, h, mine, None), ss.at[h, 1, j], rs.at[h, 1, j], a, k
                    )
                )
            c = pltpu.make_async_copy(self.source(second, h, mine, None), self.target(second, h, mine, None), self.local.at[int(second), h])
            c.start()
            self.near.append(c)

    def pass_on(self, second):
        ss, rs = (self.s2, self.r2) if second else (self.s1, self.r1)
        for h, j, k, a, c in self.far:
            c.wait_recv()
            to = self.target(second, h, self.crd(a, SIDE - k), j)
            self.near.append(self.copy(self.relay.at[int(second), h, j], to, ss.at[h, 2, j], rs.at[h, 2, j], a, k))

    def finish(self):
        for c in self.near:
            c.wait()
        for *_, c in self.far:
            c.wait_send()


def lanes_quarter(ref, half, sub):
    return ref.at[:, :, half * 512 : half * 512 + 512] if sub is None else lanes_part(ref, half * 2 + sub)


def lanes_part(ref, sub):
    return ref if sub is None else ref.at[:, :, sub * 256 : sub * 256 + 256]


def pages_quarter(ref, half, sub):
    return ref.at[:, half] if sub is None else ref.at[:, half, sub * 2 : sub * 2 + 2]


def pages_part(ref, sub):
    return ref if sub is None else ref.at[:, sub * 2 : sub * 2 + 2]


ORDER = (
    (0, 0), (1, 0), (3, 0), (0, 1), (0, 3), (2, 0), (0, 2), (1, 1),
    (1, 3), (3, 1), (3, 3), (2, 1), (2, 3), (1, 2), (3, 2), (2, 2),
)


def pick(index, values):
    out = jnp.int32(values[0])
    for i, v in enumerate(values[1:], 1):
        out = jnp.where(index == i, jnp.int32(v), out)
    return out


def attention_kernel(
    pick_ref, entry_ref, tile_ref, slot_ref, len_ref, key_ref, value_ref, q_ref, new_key_ref, new_value_ref, o_ref, *scratch
):
    page_out, page_in, page_mid, page_relay, q_in, q_mid, q_relay, far_in, far_mid, far_relay = scratch[:10]
    lse_out, lse_in, fresh, self_out, self_top, self_total, own_ref = scratch[10:17]
    blocks, q_cols, k_rows, v_cols, part, part_max, acc, acc_max, ss, rs, ps, pr, lsem = scratch[17:30]
    page_sems, q_sems, far_sems = scratch[30:35], scratch[35:40], scratch[40:45]
    small_send, small_recv, fresh_send, fresh_recv, fresh_local = scratch[45:]
    me, t = lax.axis_index("dp"), lax.axis_index("tensor")
    core = lax.rem(t, 2)
    mate = t + 1 - 2 * core
    place = (me // SIDE, me % SIDE)
    beside = {(a, k): neighbour(me, a, k) for a in (0, 1) for k in (1, 3)}
    both = (0, 1)

    barrier = pltpu.get_barrier_semaphore()
    for k in range(1, 16):
        pl.semaphore_signal(barrier, inc=1, device_id=(lax.rem(me + k, 16), t), device_id_type=MESH)
    pl.semaphore_signal(barrier, inc=1, device_id=(me, mate), device_id_type=MESH)
    for i in range(64):
        for kind, ref in enumerate((key_ref, value_ref)):
            page_out[i // 16, i // 4 % 4, kind, i % 4] = ref[pick_ref[i]]
    pl.semaphore_wait(barrier, 16)

    pages = Exchange(me, t, page_out, page_in, page_mid, page_relay, page_sems, pages_quarter, pages_part)
    spread = Exchange(me, t, q_ref, q_in, q_mid, q_relay, q_sems, lanes_quarter, lanes_part)
    pages.start(False)
    crossing = []
    for kind, ref in enumerate((new_key_ref, new_value_ref)):
        c = pltpu.make_async_remote_copy(
            src_ref=ref,
            dst_ref=fresh.at[core, kind],
            send_sem=fresh_send.at[kind],
            recv_sem=fresh_recv.at[kind],
            device_id=(me, mate),
            device_id_type=MESH,
        )
        c.start()
        crossing.append(c)
        c = pltpu.make_async_copy(ref, fresh.at[core, kind], fresh_local.at[kind])
        c.start()
        crossing.append(c)
    spread.start(False)
    for c in crossing:
        c.wait()

    count = len_ref[0]
    new_keys = jnp.concatenate([fresh[0, 0], fresh[1, 0]], axis=0)
    new_values = jnp.concatenate([fresh[0, 1], fresh[1, 1]], axis=0).T
    rows = lax.broadcasted_iota(jnp.int32, (512, 512), 0)
    cols = lax.broadcasted_iota(jnp.int32, (512, 512), 1)
    allowed = (cols <= rows) & (cols < count)

    def own_suffix(*heads):
        for h in heads:
            queries = q_ref[:, :, :, h * HD : (h + 1) * HD].reshape(512, HD)
            score = jnp.dot(queries, new_keys, preferred_element_type=jnp.float32) * SCALE
            score = jnp.where(allowed, score, FLOOR_SCORE)
            top = jnp.max(score, axis=1, keepdims=True)
            weight = jnp.exp(score - top)
            self_top[:, h : h + 1] = top
            self_total[:, h : h + 1] = jnp.sum(weight, axis=1, keepdims=True)
            self_out[h] = jnp.dot(weight.astype(jnp.bfloat16), new_values, preferred_element_type=jnp.float32)

    own_suffix(0, 1)
    pages.pass_on(False)
    own_suffix(2, 3)
    pages.finish()
    pages.start(True)
    spread.pass_on(False)
    own_suffix(4)
    spread.finish()
    spread.start(True)
    own_suffix(5)
    pages.pass_on(True)
    own_suffix(6, 7)
    pages.finish()
    for p in range(16):
        for kind in range(2):
            page = page_in[entry_ref[p], entry_ref[16 + p], kind, entry_ref[32 + p]]
            own_ref[p // 8, kind, :, p % 8 * 128 : p % 8 * 128 + 128] = page

    def number(h, i, j):
        i, j = i % SIDE, j % SIDE
        return i * SIDE + j if h == 0 else j * SIDE + i

    def block(h, i, j, kind):
        ref = blocks.at[number(h, i, j), h, core]
        return ref if kind is None else ref.at[kind]

    def origin(h, i, j, kind):
        return own_ref.at[h] if (i, j) == (0, 0) else block(h, i, j, kind)

    def hop(h, i, j, first, k, kind, group):
        to = (i - k, j) if first else (i, j - k)
        pltpu.make_async_remote_copy(
            src_ref=origin(h, i, j, kind),
            dst_ref=block(h, *to, kind),
            send_sem=ss.at[0],
            recv_sem=rs.at[group],
            device_id=(beside[h if first else 1 - h, k], t),
            device_id_type=MESH,
        ).start()

    def taken(sem, holders_of_two):
        like = blocks.at[pl.ds(0, holders_of_two), :, 0]
        pltpu.make_async_copy(like, like, sem).wait()

    def across(n):
        return pltpu.make_async_remote_copy(
            src_ref=blocks.at[n, :, core],
            dst_ref=blocks.at[n, :, core],
            send_sem=ps.at[n],
            recv_sem=pr.at[n],
            device_id=(me, mate),
            device_id_type=MESH,
        )

    def to_mate(*holders_here):
        for dx, dz in holders_here:
            across(dx * SIDE + dz).start()

    local = []
    for h in both:
        c = pltpu.make_async_copy(own_ref.at[h], blocks.at[0, h, core], lsem.at[h])
        c.start()
        local.append(c)
    for h in both:
        for k in (1, 3):
            hop(h, 0, 0, True, k, None, 0)
    for h in both:
        for k in (1, 3):
            hop(h, 0, 0, False, k, None, 1)

    def near_first():
        taken(rs.at[0], 2)
        for h in both:
            hop(h, 3, 0, True, 1, 0, 2)
            hop(h, 1, 0, True, 3, 1, 2)

    def near_second(i, group):
        for h in both:
            hop(h, i, 3, False, 1, 0, group)
            hop(h, i, 1, False, 3, 1, group)

    def own_second():
        taken(rs.at[1], 2)
        near_second(0, 3)

    def near_on():
        for h in both:
            for i in (3, 1):
                for k in (1, 3):
                    hop(h, i, 0, False, k, None, 4)

    def far_first():
        taken(rs.at[2], 1)
        for h in both:
            for k in (1, 3):
                hop(h, 2, 0, False, k, None, 6)

    def far_own():
        taken(rs.at[3], 1)
        to_mate((2, 0), (0, 2))

    def near_near():
        taken(rs.at[4], 4)
        for i in (3, 1):
            near_second(i, 5)
        to_mate((1, 1), (1, 3), (3, 1), (3, 3))

    def far_near():
        taken(rs.at[6], 2)
        near_second(2, 7)

    def near_far():
        taken(rs.at[5], 2)
        to_mate((2, 1), (2, 3), (1, 2), (3, 2))

    def far_far():
        taken(rs.at[7], 1)
        to_mate((2, 2))

    def arrived(dx, dz):
        across(dx * SIDE + dz).wait()

    numbers = [dx * SIDE + dz for dx, dz in ORDER]
    holders = [lax.rem(place[0] + dx, SIDE) * SIDE + lax.rem(place[1] + dz, SIDE) for dx, dz in ORDER]

    def prepare(n, buf):
        for m in range(2):
            for half in range(2):
                v_cols[buf, m, half * 64 : (half + 1) * 64, :] = blocks[n, m, half, 1]
            k_rows[buf, m] = jnp.concatenate([blocks[n, m, 0, 0], blocks[n, m, 1, 0]], axis=0).T

    def compute(holder, buf):
        nodes = [tile_ref[holder * 12 + 6 + i] for i in range(6)]

        def score_of(i):
            return jnp.dot(k_rows[buf, nodes[i]], q_cols[tile_ref[holder * 12 + i]], preferred_element_type=jnp.float32)

        scores = [score_of(i) for i in range(4)]
        for i in range(6):
            top = jnp.max(scores[i], axis=0, keepdims=True)
            weight = jnp.exp2(scores[i] * (SCALE * LOG2E) - top * (SCALE * LOG2E)).astype(jnp.bfloat16)
            if len(scores) < 6:
                scores.append(score_of(len(scores)))
            mixed = jnp.dot(v_cols[buf, nodes[i]], weight, preferred_element_type=jnp.float32)
            part[buf, i] = mixed[: HD + 8]
            part_max[buf, i] = jnp.broadcast_to(top * SCALE, (8, 256))

    def combine(holder, buf):
        for r in range(16):
            slot = slot_ref[holder * 32 + r]
            here = slot_ref[holder * 32 + 16 + r] > 0
            new = jnp.where(here, part_max[buf, slot], FLOOR_SCORE)
            old = acc_max[r]
            top = jnp.maximum(old, new)
            keep = jnp.exp(old - top)[:1]
            add = jnp.where(here, jnp.exp(new - top), 0.0)[:1]
            acc[r] = acc[r] * keep + part[buf, slot] * add
            acc_max[r] = top

    for c in local:
        c.wait()
    to_mate((0, 0))
    v_cols[...] = jnp.ones_like(v_cols)
    arrived(0, 0)
    prepare(0, 0)
    spread.pass_on(True)
    near_first()
    own_second()
    near_on()
    to_mate((1, 0), (3, 0), (0, 1), (0, 3))
    spread.finish()
    for r in range(16):
        rows = jnp.concatenate([q_in[r // SIDE, r % SIDE, :, g * HD : (g + 1) * HD] for g in range(8)], axis=0)
        q_cols[r] = rows.T
    acc[...] = jnp.zeros_like(acc)
    acc_max[...] = jnp.full_like(acc_max, FLOOR_SCORE)

    compute(holders[0], 0)
    arrived(*ORDER[1])
    prepare(numbers[1], 1)
    events = {1: far_first, 3: far_own, 5: near_near, 8: far_near, 9: near_far, 12: far_far}

    def step(at, _):
        for i in range(1, 15):

            @pl.when(at == i)
            def _(i=i):
                if i in events:
                    events[i]()
                arrived(*ORDER[i + 1])

        buf = at % 2
        combine(pick(at - 1, holders), 1 - buf)
        compute(pick(at, holders), buf)
        prepare(pick(at + 1, numbers + numbers[-1:]), 1 - buf)
        return 0

    lax.fori_loop(1, 16, step, 0)
    combine(holders[15], 1)
    taken(ss.at[0], 15)

    for r in range(16):
        total = acc[r, HD : HD + 1]
        some = total > 0.0
        inverse = jnp.where(some, 1.0 / jnp.where(some, total, 1.0), 0.0)
        rows = (acc[r, :HD] * inverse).T.astype(jnp.bfloat16)
        for g in range(8):
            q_in[r // SIDE, r % SIDE, :, g * HD : (g + 1) * HD] = rows[g * 32 : (g + 1) * 32]
        level = acc_max[r, :1] + jnp.log(jnp.where(some, total, 1.0))
        lse_out[r] = jnp.broadcast_to(jnp.where(some, level, FLOOR_SCORE), (8, 256))

    level_copies = []
    for k in range(1, 16):
        d = lax.rem(me + k, 16)
        c = pltpu.make_async_remote_copy(
            src_ref=lse_out.at[d],
            dst_ref=lse_in.at[me],
            send_sem=small_send.at[k],
            recv_sem=small_recv.at[k],
            device_id=(d, t),
            device_id_type=MESH,
        )
        c.start()
        level_copies.append(c)
    c = pltpu.make_async_copy(lse_out.at[me], lse_in.at[me], small_send.at[0])
    c.start()
    level_copies.append(c)
    back = Exchange(me, t, q_in, far_in, far_mid, far_relay, far_sems, lanes_quarter, lanes_part)
    for second in (False, True):
        back.start(second)
        back.pass_on(second)
        back.finish()
    for c in level_copies:
        c.wait()

    def merge(holder, _):
        here = pl.ds(pl.multiple_of(holder * 32, 32), 32)
        levels = lse_in[holder].T[:, :1]
        tops, totals = self_top[here, :], self_total[here, :]
        valid = lax.broadcasted_iota(jnp.int32, (32, HD), 0) + holder * 32 < count
        for h in range(8):
            lanes = slice(h * HD, (h + 1) * HD)
            top, total = tops[:, h : h + 1], totals[:, h : h + 1]
            level = levels[h * 32 : (h + 1) * 32]
            peak = jnp.maximum(top, level)
            keep, add = jnp.exp(top - peak), jnp.exp(level - peak)
            inverse = 1.0 / (total * keep + add)
            far = far_in[holder // SIDE, holder % SIDE, :, lanes].astype(jnp.float32)
            result = self_out[h, here] * (keep * inverse) + far * (add * inverse)
            o_ref[here, lanes] = jnp.where(valid, result, 0.0).astype(jnp.bfloat16)
        return 0

    lax.fori_loop(0, 16, merge, 0)


def attend(tables, arrays):
    vmem, smem = pl.BlockSpec(memory_space=pltpu.VMEM), pl.BlockSpec(memory_space=pltpu.SMEM)
    dma, bf16, f32 = pltpu.SemaphoreType.DMA, jnp.bfloat16, jnp.float32
    flat = (SIDE, SIDE, 32, 1024)
    exchange_sems = [dma((2, 3, 2))] * 4 + [dma((2, 2))]
    return pl.pallas_call(
        attention_kernel,
        out_shape=jax.ShapeDtypeStruct((512, 1024), bf16),
        in_specs=[smem] * len(tables) + [vmem] * len(arrays),
        out_specs=vmem,
        scratch_shapes=[
            pltpu.VMEM((SIDE, SIDE, 2, CAP, 64, 128), bf16),
            pltpu.VMEM((SIDE, SIDE, 2, CAP, 64, 128), bf16),
            pltpu.VMEM((2, SIDE, SIDE, CAP, 64, 128), bf16),
            pltpu.VMEM((2, 2, 2, SIDE, 2, 64, 128), bf16),
            pltpu.VMEM(flat, bf16),
            pltpu.VMEM((2, SIDE, SIDE, 32, 512), bf16),
            pltpu.VMEM((2, 2, 2, SIDE, 32, 256), bf16),
            pltpu.VMEM(flat, bf16),
            pltpu.VMEM((2, SIDE, SIDE, 32, 512), bf16),
            pltpu.VMEM((2, 2, 2, SIDE, 32, 256), bf16),
            pltpu.VMEM((16, 8, 256), f32),
            pltpu.VMEM((16, 8, 256), f32),
            pltpu.VMEM((2, 2, 64, 512), bf16),
            pltpu.VMEM((8, 512, HD), f32),
            pltpu.VMEM((512, HD), f32),
            pltpu.VMEM((512, HD), f32),
            pltpu.VMEM((2, 2, 64, 1024), bf16),
            pltpu.VMEM((16, 2, 2, 2, 64, 1024), bf16),
            pltpu.VMEM((16, HD, 256), bf16),
            pltpu.VMEM((2, 2, 1024, HD), bf16),
            pltpu.VMEM((2, 2, HD + 16, 1024), bf16),
            pltpu.VMEM((2, 6, HD + 8, 256), f32),
            pltpu.VMEM((2, 6, 8, 256), f32),
            pltpu.VMEM((16, HD + 8, 256), f32),
            pltpu.VMEM((16, 8, 256), f32),
            dma((1,)),
            dma((8,)),
            dma((16,)),
            dma((16,)),
            dma((2,)),
            *exchange_sems,
            *exchange_sems,
            *exchange_sems,
            dma((16,)),
            dma((16,)),
            dma((2,)),
            dma((2,)),
            dma((2,)),
        ],
        compiler_params=pltpu.CompilerParams(collective_id=1, has_side_effects=True, vmem_limit_bytes=50 * MIB),
    )(*tables, *arrays)


def body(queries, new_keys, new_values, key_cache, value_cache, page_owner, page_slot, tile_req, tile_node, suffix_len):
    dp_size = lax.axis_size("dp")
    dp_index = lax.axis_index("dp")
    owners = page_owner.reshape(dp_size, 16)
    slot_ids = page_slot.reshape(dp_size, 16)
    order = jnp.arange(16)
    same = owners[:, :, None] == owners[:, None, :]
    rank = jnp.sum(same & (order[None, :] < order[:, None])[None], axis=2, dtype=jnp.int32)
    chosen = (owners[:, :, None] == dp_index) & (rank[:, :, None] == jnp.arange(CAP)[None, None, :])
    picked = jnp.sum(jnp.where(chosen, slot_ids[:, :, None], 0), axis=1, dtype=jnp.int32).reshape(-1)
    my_owner = lax.dynamic_index_in_dim(owners, dp_index, 0, keepdims=False)
    my_rank = lax.dynamic_index_in_dim(rank, dp_index, 0, keepdims=False)
    entries = jnp.concatenate([my_owner // SIDE, my_owner % SIDE, my_rank])
    requests = tile_req.reshape(dp_size, 6)
    nodes = tile_node.reshape(dp_size, 6) - 2 * jnp.arange(dp_size, dtype=jnp.int32)[:, None]
    tiles = jnp.concatenate([requests, nodes], axis=1).reshape(-1)
    hits = requests[:, None, :] == jnp.arange(16)[None, :, None]
    slots = jnp.sum(jnp.where(hits, jnp.arange(6)[None, None, :], 0), axis=2)
    named = jnp.any(hits, axis=2)
    slots = jnp.concatenate([slots.astype(jnp.int32), named.astype(jnp.int32)], axis=1).reshape(-1)
    arrays = (
        jnp.swapaxes(key_cache, 1, 2),
        jnp.swapaxes(value_cache, 1, 2),
        queries.reshape(SIDE, SIDE, 32, 1024),
        new_keys[0].T,
        new_values[0].T,
    )
    return attend((picked, entries, tiles, slots, suffix_len), arrays)[None]


def solution(mesh):
    cut = P("dp", None, "tensor")
    return jax.shard_map(
        body,
        mesh=mesh,
        in_specs=(cut, cut, cut, cut, cut, P(), P(), P(), P(), P("dp")),
        out_specs=cut,
        check_vma=False,
    )
```

time: 167 us -> 147 us (0.88)
  Pallas kernels: 148 us -> 139 us
  local copies, waits for them, and re-layouts: 14.5 us -> 6.18 us
    pallas_call x5 -> x1, Pallas kernels: 148 us -> 139 us  [attend(): pl.pallas_call(attention_kernel, out_shape=jax.ShapeDtypeStruct((512, 102...]
    gather x3 -> x0, local copies, waits for them, and re-layouts: 5.05 us -> none  [the longest x2 2.72 us: body(): outgoing = jnp.stack([key_pages[picked], value_pages[picked]], axis=1)]
    unnamed x10 -> x19, local copies, waits for them, and re-layouts: 5.53 us -> 5.42 us
  transfers between devices with their start and end apart: 2 -> 0, of which waited for: 0 -> 0; matrix products, arithmetic and copies ran while one was open for 8% -> 0% of each run, Pallas kernels for 84% -> 0%
where the time goes in v3:
time: 147 us
  Pallas kernels  139 us (95%)
  local copies, waits for them, and re-layouts  6.18 us (4%)
    pallas_call x1, Pallas kernels, attend(): pl.pallas_call(attention_kernel, out_shape=jax.ShapeDtypeStruct((512, 102...  139 us
    unnamed x19, local copies, waits for them, and re-layouts  5.42 us

profile of v3, /device:TPU:0, one launch (start us, length us, event | category | flops | bytes accessed | tf_op | source)
XLA Modules:
  0.0 146.9 jit_solution(9580108199703657056)
XLA Ops:
  0.7 0.6 copy-done.6
  1.3 0.1 reshape.49
  1.4 0.1 copy.16
  1.5 0.1 fusion
  1.6 0.1 select_reduce_fusion
  1.7 0.1 pad_add_fusion.1
  1.8 0.1 reshape.52.slot_ref
  1.8 0.6 copy-done.7
  2.4 0.1 reshape.50
  2.5 0.1 broadcast_subtract_fusion
  2.6 0.1 pad_add_fusion
  2.7 0.1 reshape.51.tile_ref
  2.8 0.6 copy-done.4
  3.4 0.1 copy.13
  3.6 0.4 convert_reduce_fusion
  4.0 0.1 pad_add_fusion.2.entry_ref
  4.1 0.1 copy.14
  4.3 0.1 select_reduce_fusion.1
  4.4 0.1 copy.15
  4.5 0.1 reshape.48.pick_ref
  4.6 1.2 copy-done
  5.8 1.2 copy-done.1
  7.1 138.8 %shard_map.100 = bf16[512,1024]{1,0:T(8,128)(2,1)S(1)} custom-call(s32[64]{0:T(128)S(1)} %reshape.48.pick_ref, s32[48]{0:T(128)S(1)} %pad_add_fusion.2.entry_ref, s32[192]{0:T(256)S(1)} %reshape.51.tile_ref, s32[512]{0:T(512)S(1)} %reshape.52.slot_ref, s32[1]{0:T(128)S(6)} %copy.18.len_ref, bf16[64,64,128]{2,1,0:T(8,128)(2,1)S(1)} %bitcast.27, ...), custom_call_target="tpu_custom_call" | custom-call | tf_op jit(solution)/shard_map/pallas_call | solution.py:443
  145.9 1.0 copy.19
  (20 shorter events, 0.2 us)
Async XLA Ops:
  0.7 0.7 copy-start.6
  1.8 0.7 copy-start.7
  2.6 0.7 copy-start.4
  3.4 0.7 copy-start.5
  3.5 1.1 copy-start.2
  3.5 1.1 copy-start.3
  4.6 1.2 copy-start
  5.8 1.2 copy-start.1

commit v4 on v3

--- a/solution.py
+++ b/solution.py
@@ -355,6 +355,7 @@
         rows = jnp.concatenate([q_in[r // SIDE, r % SIDE, :, g * HD : (g + 1) * HD] for g in range(8)], axis=0)
         q_cols[r] = rows.T
     acc[...] = jnp.zeros_like(acc)
+    lse_out[...] = jnp.zeros_like(lse_out)
     acc_max[...] = jnp.full_like(acc_max, FLOOR_SCORE)
 
     compute(holders[0], 0)
@@ -389,7 +390,9 @@
         for g in range(8):
             q_in[r // SIDE, r % SIDE, :, g * HD : (g + 1) * HD] = rows[g * 32 : (g + 1) * 32]
         level = acc_max[r, :1] + jnp.log(jnp.where(some, total, 1.0))
-        lse_out[r] = jnp.broadcast_to(jnp.where(some, level, FLOOR_SCORE), (8, 256))
+        level = jnp.where(some, level, FLOOR_SCORE)
+        for g in range(8):
+            lse_out[r, g : g + 1, :32] = level[:, g * 32 : (g + 1) * 32]
 
     level_copies = []
     for k in range(1, 16):
@@ -417,22 +420,21 @@
 
     def merge(holder, _):
         here = pl.ds(pl.multiple_of(holder * 32, 32), 32)
-        levels = lse_in[holder].T[:, :1]
-        tops, totals = self_top[here, :], self_total[here, :]
+        levels = lse_in[holder].T[:32, :8]
+        tops, totals = self_top[here, :8], self_total[here, :8]
+        peak = jnp.maximum(tops, levels)
+        keep, add = jnp.exp(tops - peak), jnp.exp(levels - peak)
+        inverse = 1.0 / (totals * keep + add)
+        keep, add = keep * inverse, add * inverse
         valid = lax.broadcasted_iota(jnp.int32, (32, HD), 0) + holder * 32 < count
         for h in range(8):
             lanes = slice(h * HD, (h + 1) * HD)
-            top, total = tops[:, h : h + 1], totals[:, h : h + 1]
-            level = levels[h * 32 : (h + 1) * 32]
-            peak = jnp.maximum(top, level)
-            keep, add = jnp.exp(top - peak), jnp.exp(level - peak)
-            inverse = 1.0 / (total * keep + add)
             far = far_in[holder // SIDE, holder % SIDE, :, lanes].astype(jnp.float32)
-            result = self_out[h, here] * (keep * inverse) + far * (add * inverse)
+            result = self_out[h, here] * keep[:, h : h + 1] + far * add[:, h : h + 1]
             o_ref[here, lanes] = jnp.where(valid, result, 0.0).astype(jnp.bfloat16)
         return 0
 
-    lax.fori_loop(0, 16, merge, 0)
+    lax.fori_loop(0, 16, merge, 0, unroll=2)
 
 
 def attend(tables, arrays):
@@ -456,8 +458,8 @@
             pltpu.VMEM(flat, bf16),
             pltpu.VMEM((2, SIDE, SIDE, 32, 512), bf16),
             pltpu.VMEM((2, 2, 2, SIDE, 32, 256), bf16),
-            pltpu.VMEM((16, 8, 256), f32),
-            pltpu.VMEM((16, 8, 256), f32),
+            pltpu.VMEM((16, 8, 128), f32),
+            pltpu.VMEM((16, 8, 128), f32),
             pltpu.VMEM((2, 2, 64, 512), bf16),
             pltpu.VMEM((8, 512, HD), f32),
             pltpu.VMEM((512, HD), f32),

time: 147 us -> 141 us (0.959)
  Pallas kernels: 139 us -> 133 us
    pallas_call x1, Pallas kernels: 139 us -> 133 us  [attend(): pl.pallas_call(attention_kernel, out_shape=jax.ShapeDtypeStruct((512, 102...]
where the time goes in v4:
time: 141 us
  Pallas kernels  133 us (94%)
  local copies, waits for them, and re-layouts  6.18 us (4%)
    pallas_call x1, Pallas kernels, attend(): pl.pallas_call(attention_kernel, out_shape=jax.ShapeDtypeStruct((512, 102...  133 us
    unnamed x19, local copies, waits for them, and re-layouts  5.42 us

profile of v4, /device:TPU:0, one launch (start us, length us, event | category | flops | bytes accessed | tf_op | source)
XLA Modules:
  0.0 140.8 jit_solution(44553669770428425)
XLA Ops:
  0.7 0.6 copy-done.6
  1.3 0.1 reshape.49
  1.4 0.1 copy.16
  1.5 0.1 fusion
  1.6 0.1 select_reduce_fusion
  1.7 0.1 pad_add_fusion.1
  1.8 0.1 reshape.52.slot_ref
  1.8 0.6 copy-done.7
  2.4 0.1 reshape.50
  2.5 0.1 broadcast_subtract_fusion
  2.6 0.1 pad_add_fusion
  2.7 0.1 reshape.51.tile_ref
  2.8 0.6 copy-done.4
  3.4 0.1 copy.13
  3.6 0.4 convert_reduce_fusion
  4.0 0.1 pad_add_fusion.2.entry_ref
  4.1 0.1 copy.14
  4.3 0.1 select_reduce_fusion.1
  4.4 0.1 copy.15
  4.5 0.1 reshape.48.pick_ref
  4.6 1.2 copy-done
  5.8 1.2 copy-done.1
  7.1 132.7 %shard_map.100 = bf16[512,1024]{1,0:T(8,128)(2,1)S(1)} custom-call(s32[64]{0:T(128)S(1)} %reshape.48.pick_ref, s32[48]{0:T(128)S(1)} %pad_add_fusion.2.entry_ref, s32[192]{0:T(256)S(1)} %reshape.51.tile_ref, s32[512]{0:T(512)S(1)} %reshape.52.slot_ref, s32[1]{0:T(128)S(6)} %copy.18.len_ref, bf16[64,64,128]{2,1,0:T(8,128)(2,1)S(1)} %bitcast.27, ...), custom_call_target="tpu_custom_call" | custom-call | tf_op jit(solution)/shard_map/pallas_call | solution.py:445
  139.8 1.0 copy.19
  (20 shorter events, 0.2 us)
Async XLA Ops:
  0.7 0.7 copy-start.6
  1.8 0.7 copy-start.7
  2.6 0.7 copy-start.4
  3.4 0.7 copy-start.5
  3.5 1.1 copy-start.2
  3.5 1.1 copy-start.3
  4.6 1.2 copy-start
  5.8 1.2 copy-start.1
